TPU v7x, 32 devices: a whole 2x2x4 slice. The times are simulated.
32 devices in a mesh: groups: 2 (over y), trace: 4 (over z), space: 2 (over x), sub: 2 (over core).
Axes of the slice: x: 2, y: 2, z: 4, core: 2. Of those that a mesh axis runs over, the one named last changes fastest.
Arguments:
- seismic: bfloat16 [256, 1024, 128], P(('groups', 'trace', 'space', 'sub')), parts along dimension 0, may hold values from -6 to 6
- band_low: int32 [256], P('groups'), parts along dimension 0, may hold values from 0 to 127
- band_high: int32 [256], P('groups'), parts along dimension 0, may hold values from 256 to 512
- leaf_weights: bfloat16 [8, 512, 2, 64], replicated, may hold values from -0.15625 to 0.15625
- translations: float32 [32, 2, 64, 64], replicated, may hold values from -1 to 1
- level_table: int32 [3, 8, 2], replicated, may hold values from 0 to 31
Outputs:
- image_weights: float32 [16, 2, 64, 128], P(('groups', 'trace', 'space'), None, 'sub'), parts along dimension 0
There are 2 independent parts, one for each index of `groups`. A program takes and returns all parts, laid end to end along the dimension named above; an argument that names none is the same for every part. Nothing has to cross between parts.
All inputs are finite; a program needn't handle non-finite values.
Results may differ from a plain program's by a relative error of at most 0.0037.
Values may be sent and summed in bfloat16 or wider, within the bound.
A program may use at most 64 MiB of HBM per device.

v0:
```python
import math

import jax
import jax.numpy as jnp
from jax import lax
from jax.sharding import PartitionSpec as P


def swapped(x, axis, distance):
    return lax.ppermute(x, axis, [(i, i ^ 1 << distance) for i in range(lax.axis_size(axis))])


def spectral_table(freq_total, samples):
    freq_range = jnp.arange(freq_total, dtype=jnp.int32)
    time_range = jnp.arange(samples, dtype=jnp.int32)
    phase = freq_range[:, None] * time_range[None, :] % samples
    angle = phase.astype(jnp.float32) * (2.0 * math.pi / samples)
    factor = 1.0 / math.sqrt(samples)
    return (jnp.concatenate([jnp.cos(angle), -jnp.sin(angle)], axis=0) * factor).astype(
        jnp.bfloat16
    )


def complex_product(left, right):
    highest = lax.Precision.HIGHEST
    real_part = jnp.dot(left[0], right[0], precision=highest) - jnp.dot(
        left[1], right[1], precision=highest
    )
    imag_part = jnp.dot(left[0], right[1], precision=highest) + jnp.dot(
        left[1], right[0], precision=highest
    )
    return jnp.stack([real_part, imag_part])


def swap_space(weights_now, bit_no):
    return swapped(weights_now, "space", bit_no)


def swap_trace(weights_now, bit_no):
    return swapped(weights_now, "trace", bit_no)


def merge_level(
    weights_now, partner, section_no, box_index, translations, level_table, sub_place, half_rank
):
    stride = 2**section_no
    upper_flag = box_index // stride % 2 == 1
    lower_part = jnp.where(upper_flag, partner, weights_now)
    upper_part = jnp.where(upper_flag, weights_now, partner)
    entries = lax.dynamic_index_in_dim(level_table[section_no], box_index, 0, keepdims=False)
    first_mat = lax.dynamic_index_in_dim(translations, entries[0], 0, keepdims=False)
    second_mat = lax.dynamic_index_in_dim(translations, entries[1], 0, keepdims=False)
    full_lower, full_upper = (
        lax.all_gather(lower_part, "sub", axis=1, tiled=True),
        lax.all_gather(upper_part, "sub", axis=1, tiled=True),
    )
    first_rows = lax.dynamic_slice_in_dim(first_mat, sub_place * half_rank, half_rank, 1)
    second_rows = lax.dynamic_slice_in_dim(second_mat, sub_place * half_rank, half_rank, 1)
    return complex_product(first_rows, full_lower) + complex_product(second_rows, full_upper)


def join_complex(parts):
    return jnp.stack([parts[:, 0, 0] - parts[:, 1, 1], parts[:, 0, 1] + parts[:, 1, 0]], axis=1)


def per_device(seismic, band_low, band_high, leaf_weights, translations, level_table):
    highest = lax.Precision.HIGHEST
    trace_count = lax.axis_size("trace")
    space_count = lax.axis_size("space")
    sub_count = lax.axis_size("sub")
    trace_place = lax.axis_index("trace")
    space_place = lax.axis_index("space")
    sub_place = lax.axis_index("sub")
    traces_here = seismic.shape[0]
    samples = seismic.shape[1]
    shots_count = seismic.shape[2]
    freq_total = leaf_weights.shape[1]
    rank_total = leaf_weights.shape[3]
    freq_block = freq_total // trace_count
    half_rank = rank_total // sub_count
    dft_rows = spectral_table(freq_total, samples)
    spectra = jnp.einsum(
        "kt,xts->xks", dft_rows, seismic, preferred_element_type=jnp.float32
    ).astype(jnp.bfloat16)
    spectra = spectra.reshape(traces_here, 2, freq_total, shots_count)
    freq_index = jnp.arange(freq_total, dtype=jnp.int32)
    band_mask = (
        (freq_index[:, None] >= band_low[None, :]) & (freq_index[:, None] < band_high[None, :])
    ).astype(jnp.bfloat16)
    masked = spectra * band_mask
    piece = masked.astype(jnp.float32)
    piece = piece.reshape(traces_here, 2, 1 * lax.axis_size("trace"), freq_block, shots_count)
    leaf_piece = leaf_weights.astype(jnp.float32)
    leaf_piece = leaf_piece.reshape(
        traces_here, 1 * lax.axis_size("trace"), freq_block, 2, rank_total
    )
    parts = jnp.einsum("iagfs,igfbr->gabrs", piece, leaf_piece, precision=highest)
    leaf_terms = lax.psum_scatter(join_complex(parts), "trace", scatter_dimension=0, tiled=True)[0]
    weights_now = lax.psum_scatter(leaf_terms, "sub", scatter_dimension=1, tiled=True)
    box_index = trace_place * space_count + space_place
    section_no = 0
    for bit_no in range(space_count.bit_length() - 1):
        partner = swap_space(weights_now, bit_no)
        weights_now = merge_level(
            weights_now,
            partner,
            section_no,
            box_index,
            translations,
            level_table,
            sub_place,
            half_rank,
        )
        section_no = section_no + 1
    for bit_no in range(trace_count.bit_length() - 1):
        partner = swap_trace(weights_now, bit_no)
        weights_now = merge_level(
            weights_now,
            partner,
            section_no,
            box_index,
            translations,
            level_table,
            sub_place,
            half_rank,
        )
        section_no = section_no + 1
    return weights_now[None]


def solution(mesh):
    placed = (
        P(("groups", "trace", "space", "sub"), None, None),
        P("groups"),
        P("groups"),
        P(),
        P(),
        P(),
    )
    return jax.shard_map(
        per_device,
        mesh=mesh,
        in_specs=placed,
        out_specs=P(("groups", "trace", "space"), None, "sub", None),
        check_vma=False,
    )
```

profile of v0, /device:TPU:0, one launch (start us, length us, event | category | flops | bytes accessed | tf_op | source)
XLA Modules:
  0.0 130.0 jit_solution(6518825922546346239)
XLA Ops:
  6.5 9.2 %sine_negate_fusion = (f32[512,1024]{1,0:T(8,128)}, f32[512,1024]{1,0:T(8,128)}) fusion(), kind=kLoop, calls=%fused_computation.14 | loop fusion | flops 7864320 | bytes 4194304 | tf_op jit(solution)/shard_map/neg | solution.py:19
  15.7 1.1 reshape.198
  16.9 4.6 %fusion.13 = bf16[1024,8,128]{2,0,1:T(8,128)(2,1)S(1)} fusion(bf16[8,1024,128]{2,1,0:T(8,128)(2,1)S(1)} %copy-done, f32[512,1024]{1,0:T(8,128)} %get-tuple-element.22, f32[512,1024]{1,0:T(8,128)} %get-tuple-element.23), kind=kOutput, calls=%fused_computation.18 | convolution fusion | flops 2151677952 | bytes 8388608 | tf_op jit(solution)/shard_map/kt,xts->xks/dot_general | solution.py:82
  21.5 0.1 and_convert_fusion
  21.7 0.6 fusion.16
  22.4 0.7 pad_maximum_fusion
  23.2 0.6 dynamic-slice.15
  23.8 37.5 %all-reduce.3.cloned.1.call-done = f32[4,2,64,128]{3,2,0,1:T(8,128)} async-done(((f32[4,2,64,128]{3,2,0,1:T(8,128)}), f32[4,2,64,128]{3,2,0,1:T(8,128)}) %all-reduce.3.cloned.1.call-update) | async-done | bytes 262160
  61.3 2.1 %dynamic-slice_bitcast_fusion = f32[2,64,128]{2,1,0:T(8,128)} fusion(f32[4,2,64,128]{3,2,0,1:T(8,128)} %all-reduce.3.cloned.1.call-done, u32[]{:T(128)} %bitcast.63), kind=kLoop, calls=%fused_computation.55 | loop fusion | bytes 131076 | tf_op jit(solution)/shard_map/squeeze | solution.py:98
  63.5 0.5 fusion.78
  64.1 6.7 %reduce-scatter.5.cloned.1.call-done = f32[2,32,128]{2,1,0:T(8,128)} async-done(((f32[2,64,128]{2,1,0:T(8,128)}), f32[2,32,128]{2,1,0:T(8,128)}) %reduce-scatter.5.cloned.1.call-update) | async-done | bytes 32784 | tf_op jit(solution)/shard_map/reduce_scatter | solution.py:99
  70.8 1.7 %collective-permute-start = (f32[2,32,128]{2,1,0:T(8,128)}, f32[2,32,128]{2,1,0:T(8,128)S(1)}, u32[]{:S(2)}, u32[]{:S(2)}) collective-permute-start(f32[2,32,128]{2,1,0:T(8,128)} %reduce-scatter.5.cloned.1.call-done), channel_id=1, source_target_pairs={{0,2},{2,0},{1,3},{3,1},{4,6},{6,4},{5,7},{7,5},{8,10},{10,8},{9,1... | collective-permute-start | bytes 98312 | tf_op jit(solution)/shard_map/ppermute | solution.py:10
  72.5 0.6 fusion.77
  76.9 0.8 broadcast_select_fusion
  77.7 1.8 %all_gather.18 = f32[2,64,128]{2,1,0:T(8,128)S(1)} all-gather(f32[2,32,128]{2,1,0:T(8,128)S(1)} %get-tuple-element.10), channel_id=1, replica_groups=mesh['groups'=2,'trace'=4,'space'=2,'sub'=2] {'sub'}, dimensions={1}, use_global_device_ids=true | all-gather | bytes 98304 | tf_op jit(solution)/shard_map/all_gather | solution.py:54
  79.5 0.9 fusion.37
  80.4 0.9 fusion.38
  81.3 1.9 %all_gather.19 = f32[2,64,128]{2,1,0:T(8,128)S(1)} all-gather(f32[2,32,128]{2,1,0:T(8,128)S(1)} %get-tuple-element.9), channel_id=1, replica_groups=mesh['groups'=2,'trace'=4,'space'=2,'sub'=2] {'sub'}, dimensions={1}, use_global_device_ids=true | all-gather | bytes 98304 | tf_op jit(solution)/shard_map/all_gather | solution.py:55
  83.2 0.9 fusion.39
  84.0 0.9 fusion.40
  84.9 0.9 fusion.29
  85.8 0.9 fusion.30
  86.7 0.9 fusion.27
  87.6 0.9 fusion.28
  88.5 1.5 %collective-permute-start.1 = (f32[2,32,128]{2,1,0:T(8,128)S(1)}, f32[2,32,128]{2,1,0:T(8,128)S(1)}, u32[]{:S(2)}, u32[]{:S(2)}) collective-permute-start(f32[2,32,128]{2,1,0:T(8,128)S(1)} %maximum_add_fusion), channel_id=1, source_target_pairs={{0,4},{4,0},{8,12},{12,8},{1,5},{5,1},{9,13},{13,9},{2,6},{6,2},{1... | collective-permute-start | bytes 98312 | tf_op jit(solution)/shard_map/ppermute | solution.py:10
  93.9 1.9 %all_gather.20 = f32[2,64,128]{2,1,0:T(8,128)S(1)} all-gather(f32[2,32,128]{2,1,0:T(8,128)S(1)} %get-tuple-element.8), channel_id=1, replica_groups=mesh['groups'=2,'trace'=4,'space'=2,'sub'=2] {'sub'}, dimensions={1}, use_global_device_ids=true | all-gather | bytes 98304 | tf_op jit(solution)/shard_map/all_gather | solution.py:54
  95.7 0.9 fusion.41
  96.6 0.9 fusion.42
  97.5 1.9 %all_gather.21 = f32[2,64,128]{2,1,0:T(8,128)S(1)} all-gather(f32[2,32,128]{2,1,0:T(8,128)S(1)} %get-tuple-element.7), channel_id=1, replica_groups=mesh['groups'=2,'trace'=4,'space'=2,'sub'=2] {'sub'}, dimensions={1}, use_global_device_ids=true | all-gather | bytes 98304 | tf_op jit(solution)/shard_map/all_gather | solution.py:55
  99.3 0.9 fusion.43
  100.2 0.9 fusion.44
  101.1 0.9 fusion.25
  102.0 0.9 fusion.26
  102.9 0.9 fusion.23
  103.8 0.9 fusion.24
  104.7 2.5 %collective-permute-start.2 = (f32[2,32,128]{2,1,0:T(8,128)S(1)}, f32[2,32,128]{2,1,0:T(8,128)S(1)}, u32[]{:S(2)}, u32[]{:S(2)}) collective-permute-start(f32[2,32,128]{2,1,0:T(8,128)S(1)} %maximum_add_fusion.1), channel_id=1, source_target_pairs={{0,8},{4,12},{8,0},{12,4},{1,9},{5,13},{9,1},{13,5},{2,10},{6,14},... | collective-permute-start | bytes 98312 | tf_op jit(solution)/shard_map/ppermute | solution.py:10
  107.1 0.6 fusion.76
  111.8 1.9 %all_gather.22 = f32[2,64,128]{2,1,0:T(8,128)S(1)} all-gather(f32[2,32,128]{2,1,0:T(8,128)S(1)} %get-tuple-element.6), channel_id=1, replica_groups=mesh['groups'=2,'trace'=4,'space'=2,'sub'=2] {'sub'}, dimensions={1}, use_global_device_ids=true | all-gather | bytes 98304 | tf_op jit(solution)/shard_map/all_gather | solution.py:54
  113.6 0.9 fusion.45
  114.5 0.9 fusion.46
  115.4 1.9 %all_gather.23 = f32[2,64,128]{2,1,0:T(8,128)S(1)} all-gather(f32[2,32,128]{2,1,0:T(8,128)S(1)} %get-tuple-element.5), channel_id=1, replica_groups=mesh['groups'=2,'trace'=4,'space'=2,'sub'=2] {'sub'}, dimensions={1}, use_global_device_ids=true | all-gather | bytes 98304 | tf_op jit(solution)/shard_map/all_gather | solution.py:55
  117.2 0.9 fusion.47
  118.1 0.9 fusion.48
  119.0 0.9 fusion.21
  119.9 0.9 fusion.22
  120.8 0.9 fusion.19
  121.7 0.9 fusion.20
  122.5 0.6 maximum_add_fusion.2
  (31 shorter events, 0.3 us)
Async XLA Ops:
  6.5 10.3 %copy-start = (bf16[8,1024,128]{2,1,0:T(8,128)(2,1)S(1)}, bf16[8,1024,128]{2,1,0:T(8,128)(2,1)}, u32[]{:S(2)}) copy-start(bf16[8,1024,128]{2,1,0:T(8,128)(2,1)} %param.6) | copy-start | bytes 6291460
  6.5 9.2 %copy-start.1 = (bf16[8,512,2,64]{1,3,2,0:T(8,128)(2,1)S(1)}, bf16[8,512,2,64]{1,3,2,0:T(8,128)(2,1)}, u32[]{:S(2)}) copy-start(bf16[8,512,2,64]{1,3,2,0:T(8,128)(2,1)} %param.9) | copy-start | bytes 3145732
  6.5 54.8 %all-reduce.3.cloned.1.call-start = ((), (), s32[]{:S(2)}) async-start(), calls=%async_computation.2 | async-start | bytes 524288
  16.9 4.7 %copy-start.4 = (s32[128]{0:T(128)S(1)}, s32[128]{0:T(128)}, u32[]{:S(2)}) copy-start(s32[128]{0:T(128)} %param.8) | copy-start | bytes 1540
  16.9 4.7 %copy-start.5 = (s32[128]{0:T(128)S(1)}, s32[128]{0:T(128)}, u32[]{:S(2)}) copy-start(s32[128]{0:T(128)} %param.7) | copy-start | bytes 1540
  16.9 4.8 %copy-start.2 = (bf16[8,4,128,2,64]{2,1,4,3,0:T(4,128)(2,1)S(1)}, bf16[8,4,128,2,64]{2,1,4,3,0:T(4,128)(2,1)}, u32[]{:S(2)}) copy-start(bf16[8,4,128,2,64]{2,1,4,3,0:T(4,128)(2,1)} %reshape.198) | copy-start | bytes 3145732
  21.7 1.5 %copy-start.6 = (u32[32]{0:T(128)S(1)}, u32[32]{0:T(128)}, u32[]{:S(2)}) copy-start(u32[32]{0:T(128)} %constant.238) | copy-start | bytes 388
  21.7 2.1 %copy-start.3 = (s32[3,8,2]{1,2,0:T(2,128)S(1)}, s32[3,8,2]{1,2,0:T(2,128)}, u32[]{:S(2)}) copy-start(s32[3,8,2]{1,2,0:T(2,128)} %param.11) | copy-start | bytes 580
  23.1 47.7 %reduce-scatter.5.cloned.1.call-start = ((), (), s32[]{:S(2)}) async-start(), calls=%async_computation.1 | async-start | bytes 98304 | tf_op jit(solution)/shard_map/reduce_scatter | solution.py:99
  70.8 6.1 %collective-permute-start = (f32[2,32,128]{2,1,0:T(8,128)}, f32[2,32,128]{2,1,0:T(8,128)S(1)}, u32[]{:S(2)}, u32[]{:S(2)}) collective-permute-start(f32[2,32,128]{2,1,0:T(8,128)} %reduce-scatter.5.cloned.1.call-done), channel_id=1, source_target_pairs={{0,2},{2,0},{1,3},{3,1},{4,6},{6,4},{5,7},{7,5},{8,10},{10,8},{9,1... | collective-permute-start | bytes 98312 | tf_op jit(solution)/shard_map/ppermute | solution.py:10
  88.5 5.4 %collective-permute-start.1 = (f32[2,32,128]{2,1,0:T(8,128)S(1)}, f32[2,32,128]{2,1,0:T(8,128)S(1)}, u32[]{:S(2)}, u32[]{:S(2)}) collective-permute-start(f32[2,32,128]{2,1,0:T(8,128)S(1)} %maximum_add_fusion), channel_id=1, source_target_pairs={{0,4},{4,0},{8,12},{12,8},{1,5},{5,1},{9,13},{13,9},{2,6},{6,2},{1... | collective-permute-start | bytes 98312 | tf_op jit(solution)/shard_map/ppermute | solution.py:10
  104.7 7.1 %collective-permute-start.2 = (f32[2,32,128]{2,1,0:T(8,128)S(1)}, f32[2,32,128]{2,1,0:T(8,128)S(1)}, u32[]{:S(2)}, u32[]{:S(2)}) collective-permute-start(f32[2,32,128]{2,1,0:T(8,128)S(1)} %maximum_add_fusion.1), channel_id=1, source_target_pairs={{0,8},{4,12},{8,0},{12,4},{1,9},{5,13},{9,1},{13,5},{2,10},{6,14},... | collective-permute-start | bytes 98312 | tf_op jit(solution)/shard_map/ppermute | solution.py:10
Sparse Core Ops, SparseCore 0:
  23.2 38.0 all-reduce.2
  63.6 7.1 reduce-scatter.4
where the time goes:
time: 133 us; the launch traced here: 130 us
  waiting for transfers between devices  44.3 us (33%)
  matrix products  26.3 us (20%)
  between operations  25.3 us (19%)
  other arithmetic  11.5 us (9%)
  blocking collectives  11.1 us (8%)
  starting transfers between devices  5.79 us (4%)
  local copies, waits for them, and re-layouts  5.69 us (4%)
    unnamed x3, waiting for transfers between devices  37.6 us
    neg x1, other arithmetic, spectral_table(): -jnp.sin(angle)  9.19 us
    reduce_scatter x1, waiting for transfers between devices, per_device(): lax.psum_scatter(leaf_terms, 'sub', scatter_dimension=1, tiled=True)  6.74 us
    ppermute x3, starting transfers between devices, swapped(): lax.ppermute(x, axis, [(i, i ^ 1 << distance) for i in range(lax.axis_siz...  5.75 us
    all_gather x3, blocking collectives, merge_level(): lax.all_gather(upper_part, 'sub', axis=1, tiled=True)  5.57 us
    all_gather x3, blocking collectives, merge_level(): lax.all_gather(lower_part, 'sub', axis=1, tiled=True)  5.55 us
    dot_general x6, matrix products, complex_product(): jnp.dot(left[1], right[1], precision=highest)  5.29 us
    dot_general x6, matrix products, complex_product(): jnp.dot(left[0], right[1], precision=highest)  5.28 us
  transfers between devices with their start and end apart: 5, of which 2 were waited for; matrix products, arithmetic and copies ran while one was open for 2% of the time, Pallas kernels for 0%

commit v1 on v0

--- a/solution.py
+++ b/solution.py
@@ -1,9 +1,16 @@
+import functools
 import math
 
 import jax
 import jax.numpy as jnp
+import ml_dtypes
+import numpy as np
 from jax import lax
+from jax.experimental import pallas as pl
+from jax.experimental.pallas import tpu as pltpu
 from jax.sharding import PartitionSpec as P
+
+LANES = 128
 
 
 def swapped(x, axis, distance):
@@ -63,7 +70,7 @@
     return jnp.stack([parts[:, 0, 0] - parts[:, 1, 1], parts[:, 0, 1] + parts[:, 1, 0]], axis=1)
 
 
-def per_device(seismic, band_low, band_high, leaf_weights, translations, level_table):
+def general_device(seismic, band_low, band_high, leaf_weights, translations, level_table):
     highest = lax.Precision.HIGHEST
     trace_count = lax.axis_size("trace")
     space_count = lax.axis_size("space")
@@ -128,6 +135,329 @@
     return weights_now[None]
 
 
+def table_rows(freq_total, samples, chunks):
+    phase = np.arange(freq_total)[:, None] * np.arange(samples)[None, :] % samples
+    angle = phase.astype(np.float32) * np.float32(2.0 * math.pi / samples)
+    factor = np.float32(1.0 / math.sqrt(samples))
+    parts = np.stack([np.cos(angle), -np.sin(angle)]) * factor
+    rows = parts.reshape(2, chunks, freq_total // chunks, samples).transpose(1, 0, 2, 3)
+    return rows.reshape(chunks, 2 * freq_total // chunks, samples).astype(ml_dtypes.bfloat16)
+
+
+def split_two(x):
+    high = x.astype(jnp.bfloat16).astype(jnp.float32)
+    return high, x - high
+
+
+def fused_kernel(
+    sizes,
+    x_hbm,
+    low_ref,
+    high_ref,
+    q_hbm,
+    tab_hbm,
+    tr_hbm,
+    level_ref,
+    out_ref,
+    x_v,
+    q_v,
+    tab_v,
+    tr_v,
+    spec_v,
+    mat_hi,
+    mat_lo,
+    send1,
+    recv1,
+    send2,
+    recv2,
+    load_sem,
+    send_sem1,
+    recv_sem1,
+    send_sem2,
+    recv_sem2,
+):
+    trace_count, space_count, sub_count = sizes
+    devices = trace_count * space_count * sub_count
+    t, p, u = lax.axis_index("trace"), lax.axis_index("space"), lax.axis_index("sub")
+    me = (t * space_count + p) * sub_count + u
+    chunks = tab_v.shape[0]
+    traces = q_v.shape[0]
+    pairs = traces // 2
+    bands = trace_count // chunks
+    boxes = trace_count * space_count
+    levels = mat_hi.shape[0]
+    rank = tr_v.shape[2]
+    half = rank // sub_count
+    block = LANES // devices
+
+    loads = []
+    for h in range(chunks):
+        loads.append(pltpu.make_async_copy(tab_hbm.at[h], tab_v.at[h], load_sem.at[len(loads)]))
+    x_loads = []
+    for j in range(traces):
+        x_loads.append(
+            pltpu.make_async_copy(
+                x_hbm.at[j],
+                x_v.at[j // 2, :, pl.ds(j % 2 * LANES, LANES)],
+                load_sem.at[chunks + j],
+            )
+        )
+    q_load = pltpu.make_async_copy(q_hbm, q_v, load_sem.at[chunks + traces])
+    tr_load = pltpu.make_async_copy(tr_hbm, tr_v, load_sem.at[chunks + traces + 1])
+    loads[0].start()
+    for load in x_loads:
+        load.start()
+    q_load.start()
+    for load in loads[1:]:
+        load.start()
+    tr_load.start()
+
+    offsets = [
+        (dt, dp, du)
+        for dt in range(trace_count)
+        for dp in range(space_count)
+        for du in range(sub_count)
+        if dt or dp or du
+    ]
+    offsets.sort(key=lambda o: -min(o[0], trace_count - o[0]) * 4 - o[1] * 2 - o[2])
+
+    def place(offset):
+        dt, dp, du = offset
+        tt = lax.rem(t + dt, trace_count)
+        pp = lax.rem(p + dp, space_count)
+        uu = lax.rem(u + du, sub_count)
+        return tt, pp, uu
+
+    barrier = pltpu.get_barrier_semaphore()
+    for offset in offsets:
+        tt, pp, uu = place(offset)
+        pl.semaphore_signal(
+            barrier,
+            inc=1,
+            device_id={"trace": tt, "space": pp, "sub": uu},
+            device_id_type=pl.DeviceIdType.MESH,
+        )
+
+    copies1 = []
+    for h in range(chunks):
+        loads[h].wait()
+        width = bands * LANES
+        freq = lax.broadcasted_iota(jnp.int32, (width, LANES), 0) + h * width
+        keep = (freq >= low_ref[...]) & (freq < high_ref[...])
+        for pair in range(pairs):
+            if h == 0:
+                x_loads[2 * pair].wait()
+                x_loads[2 * pair + 1].wait()
+            rows = jnp.dot(tab_v[h], x_v[pair], preferred_element_type=jnp.float32)
+            for part in range(2):
+                for k in range(2):
+                    piece = rows[part * width : (part + 1) * width, k * LANES : (k + 1) * LANES]
+                    piece = jnp.where(keep, piece, 0.0).astype(jnp.bfloat16)
+                    j = 2 * pair + k
+                    for g in range(bands):
+                        spec_v[
+                            h * bands + g,
+                            j * LANES : (j + 1) * LANES,
+                            part * LANES : (part + 1) * LANES,
+                        ] = piece[g * LANES : (g + 1) * LANES]
+        if h == 0:
+            q_load.wait()
+        leaves = []
+        for g in range(h * bands, (h + 1) * bands):
+            left = jnp.concatenate(
+                [q_v[j, :, g * LANES : (g + 1) * LANES] for j in range(traces)], axis=1
+            )
+            both = jnp.dot(left, spec_v[g], preferred_element_type=jnp.float32)
+            real = both[:rank, :LANES] - both[rank:, LANES:]
+            imag = both[rank:, :LANES] + both[:rank, LANES:]
+            turned = jnp.concatenate([real, imag], axis=0).T
+            leaves.append(turned.reshape(devices, block, LANES))
+        send1[h] = jnp.concatenate(leaves, axis=1).astype(jnp.bfloat16)
+        if h == 0:
+            pl.semaphore_wait(barrier, devices - 1)
+        for i, offset in enumerate(offsets):
+            tt, pp, uu = place(offset)
+            copy = pltpu.make_async_remote_copy(
+                src_ref=send1.at[h, (tt * space_count + pp) * sub_count + uu],
+                dst_ref=recv1.at[h, i],
+                send_sem=send_sem1.at[h, i],
+                recv_sem=recv_sem1.at[h, i],
+                device_id={"trace": tt, "space": pp, "sub": uu},
+                device_id_type=pl.DeviceIdType.MESH,
+            )
+            copy.start()
+            copies1.append(copy)
+
+    tr_load.wait()
+    for level in range(levels):
+        stride = 2**level
+        lowers = [b for b in range(boxes) if b // stride % 2 == 0]
+        for q, lower in enumerate(lowers):
+            for side in range(2):
+                for child in range(2):
+                    entry = level_ref[level, child, lower + side * stride]
+                    real, imag = tr_v[entry, 0], tr_v[entry, 1]
+                    top = jnp.concatenate([real, -imag], axis=1)
+                    bottom = jnp.concatenate([imag, real], axis=1)
+                    for part, rows in enumerate((top, bottom)):
+                        high, rest = split_two(rows)
+                        high, rest = high.astype(jnp.bfloat16), rest.astype(jnp.bfloat16)
+                        columns = slice(child * LANES, (child + 1) * LANES)
+                        if level < levels - 1:
+                            at = side * 2 * rank + part * rank
+                            mat_hi[level, q, at : at + rank, columns] = high
+                            mat_lo[level, q, at : at + rank, columns] = rest
+                        else:
+                            for s in range(sub_count):
+                                at = s * 4 * half + side * 2 * half + part * half
+                                mine = slice(s * half, (s + 1) * half)
+                                mat_hi[level, q, at : at + half, columns] = high[mine]
+                                mat_lo[level, q, at : at + half, columns] = rest[mine]
+
+    same = [send1[h, me].astype(jnp.float32) for h in range(chunks)]
+    other = [None] * chunks
+    for h in range(chunks):
+        for i, offset in enumerate(offsets):
+            copies1[h * len(offsets) + i].wait_recv()
+            got = recv1[h, i].astype(jnp.float32)
+            if offset[1] == 0:
+                same[h] = same[h] + got
+            else:
+                other[h] = got if other[h] is None else other[h] + got
+    first = p == 0
+    now = [None] * boxes
+    for h in range(chunks):
+        for place_no in range(space_count):
+            total = jnp.where(first == (place_no == 0), same[h], other[h])
+            for g in range(bands):
+                box = (h * bands + g) * space_count + place_no
+                now[box] = total[g * block : (g + 1) * block]
+
+    for level in range(levels):
+        stride = 2**level
+        lowers = [b for b in range(boxes) if b // stride % 2 == 0]
+        for q, lower in enumerate(lowers):
+            both = jnp.concatenate([now[lower], now[lower + stride]], axis=1)
+            left = jnp.concatenate(split_two(both), axis=0).astype(jnp.bfloat16)
+            dims = (((1,), (1,)), ((), ()))
+            main = lax.dot_general(
+                left, mat_hi[level, q], dims, preferred_element_type=jnp.float32
+            )
+            rest = lax.dot_general(
+                left, mat_lo[level, q], dims, preferred_element_type=jnp.float32
+            )
+            joined = main[:block] + (main[block:] + rest[:block])
+            if level < levels - 1:
+                now[lower], now[lower + stride] = joined[:, :LANES], joined[:, LANES:]
+            else:
+                for s in range(sub_count):
+                    send2[q * sub_count + s] = joined[:, s * LANES : (s + 1) * LANES]
+
+    copies2 = []
+    for i, offset in enumerate(offsets):
+        tt, pp, uu = place(offset)
+        copy = pltpu.make_async_remote_copy(
+            src_ref=send2.at[lax.rem(tt * space_count + pp, boxes // 2) * sub_count + uu],
+            dst_ref=recv2.at[me],
+            send_sem=send_sem2.at[i],
+            recv_sem=recv_sem2.at[i],
+            device_id={"trace": tt, "space": pp, "sub": uu},
+            device_id_type=pl.DeviceIdType.MESH,
+        )
+        copy.start()
+        copies2.append(copy)
+    mine = t * space_count + p
+    recv2[me] = send2[lax.rem(mine, boxes // 2) * sub_count + u]
+    for copy in copies2:
+        copy.wait_recv()
+    turned = recv2[...].reshape(LANES, LANES).T
+    upper = mine >= boxes // 2
+    chosen = jnp.where(upper, turned[2 * half :], turned[: 2 * half])
+    out_ref[...] = chosen.reshape(1, 2, half, LANES)
+    for copy in copies1 + copies2:
+        copy.wait_send()
+
+
+def fused_device(seismic, band_low, band_high, leaf_weights, translations, level_table):
+    sizes = tuple(lax.axis_size(name) for name in ("trace", "space", "sub"))
+    devices = math.prod(sizes)
+    boxes = sizes[0] * sizes[1]
+    traces, samples, shots = seismic.shape
+    freq_total, rank = leaf_weights.shape[1], leaf_weights.shape[3]
+    chunks = 2
+    levels = level_table.shape[0]
+    table = jnp.asarray(table_rows(freq_total, samples, chunks))
+    weights = leaf_weights.transpose(0, 2, 3, 1).reshape(traces, 2 * rank, freq_total)
+    block = shots // devices
+    rows = sizes[0] // chunks * block
+    any_spec = pl.BlockSpec(memory_space=pl.ANY)
+    vmem_spec = pl.BlockSpec(memory_space=pltpu.VMEM)
+    dma = pltpu.SemaphoreType.DMA
+    return pl.pallas_call(
+        functools.partial(fused_kernel, sizes),
+        out_shape=jax.ShapeDtypeStruct((1, 2, rank // sizes[2], shots), jnp.float32),
+        in_specs=[
+            any_spec,
+            vmem_spec,
+            vmem_spec,
+            any_spec,
+            any_spec,
+            any_spec,
+            pl.BlockSpec(memory_space=pltpu.SMEM),
+        ],
+        out_specs=vmem_spec,
+        scratch_shapes=[
+            pltpu.VMEM((traces // 2, samples, 2 * shots), jnp.bfloat16),
+            pltpu.VMEM(weights.shape, jnp.bfloat16),
+            pltpu.VMEM(table.shape, jnp.bfloat16),
+            pltpu.VMEM(translations.shape, jnp.float32),
+            pltpu.VMEM((sizes[0], traces * LANES, 2 * LANES), jnp.bfloat16),
+            pltpu.VMEM((levels, boxes // 2, 4 * rank, 4 * rank), jnp.bfloat16),
+            pltpu.VMEM((levels, boxes // 2, 4 * rank, 4 * rank), jnp.bfloat16),
+            pltpu.VMEM((chunks, devices, rows, LANES), jnp.bfloat16),
+            pltpu.VMEM((chunks, devices - 1, rows, LANES), jnp.bfloat16),
+            pltpu.VMEM((boxes // 2 * sizes[2], block, LANES), jnp.float32),
+            pltpu.VMEM((devices, block, LANES), jnp.float32),
+            dma((chunks + traces + 2,)),
+            dma((chunks, devices - 1)),
+            dma((chunks, devices - 1)),
+            dma((devices - 1,)),
+            dma((devices - 1,)),
+        ],
+        compiler_params=pltpu.CompilerParams(
+            collective_id=0, has_side_effects=True, vmem_limit_bytes=40 * 2**20
+        ),
+    )(
+        seismic,
+        band_low.reshape(1, shots),
+        band_high.reshape(1, shots),
+        weights,
+        table,
+        translations,
+        level_table.transpose(0, 2, 1),
+    )
+
+
+def per_device(seismic, band_low, band_high, leaf_weights, translations, level_table):
+    trace_count, space_count, sub_count = (
+        lax.axis_size(name) for name in ("trace", "space", "sub")
+    )
+    devices = trace_count * space_count * sub_count
+    traces, _, shots = seismic.shape
+    freq_total, rank = leaf_weights.shape[1], leaf_weights.shape[3]
+    fits = (
+        shots == LANES
+        and shots == 8 * devices
+        and freq_total == trace_count * LANES
+        and 2 * rank == LANES
+        and 4 * rank == LANES * sub_count
+        and traces % 2 == 0
+        and trace_count % 2 == 0
+    )
+    chosen = fused_device if fits else general_device
+    return chosen(seismic, band_low, band_high, leaf_weights, translations, level_table)
+
+
 def solution(mesh):
     placed = (
         P(("groups", "trace", "space", "sub"), None, None),

time: 133 us -> 28.4 us (0.21); the launches traced: 130 us -> 28.1 us
  waiting for transfers between devices: 44.3 us -> 0 us
  matrix products: 26.3 us -> 0 us
  between operations: 25.3 us -> 0.02 us
  Pallas kernels: 0 us -> 19.5 us
  other arithmetic: 11.5 us -> 0 us
  blocking collectives: 11.1 us -> 0 us
  starting transfers between devices: 5.79 us -> 0 us
  local copies, waits for them, and re-layouts: 5.69 us -> 8.61 us
    unnamed x3 -> x0, waiting for transfers between devices: 37.6 us -> none
    dot_general x26 -> x0, matrix products: 26.3 us -> none  [the longest x6 5.29 us: complex_product(): jnp.dot(left[1], right[1], precision=highest)]
    pallas_call x0 -> x1, Pallas kernels: none -> 19.5 us  [fused_device(): pl.pallas_call(functools.partial(fused_kernel, sizes), out_shape=jax.Shap...]
    all_gather x6 -> x0, blocking collectives: 11.1 us -> none  [the longest x3 5.57 us: merge_level(): lax.all_gather(upper_part, 'sub', axis=1, tiled=True)]
    neg x1 -> x0, other arithmetic: 9.19 us -> none  [spectral_table(): -jnp.sin(angle)]
    unnamed x15, local copies, waits for them, and re-layouts: 0.62 us -> 8.61 us
    reduce_scatter x1 -> x0, waiting for transfers between devices: 6.74 us -> none  [per_device(): lax.psum_scatter(leaf_terms, 'sub', scatter_dimension=1, tiled=True)]
    ppermute x3 -> x0, starting transfers between devices: 5.75 us -> none  [swapped(): lax.ppermute(x, axis, [(i, i ^ 1 << distance) for i in range(lax.axis_siz...]
  transfers between devices with their start and end apart: 5 -> 0, of which waited for: 2 -> 0; matrix products, arithmetic and copies ran while one was open for 2% -> 0% of each run, Pallas kernels for 0% -> 0%
where the time goes in v1:
time: 28.4 us; the launch traced here: 28.1 us
  Pallas kernels  19.5 us (69%)
  local copies, waits for them, and re-layouts  8.61 us (30%)
    pallas_call x1, Pallas kernels, fused_device(): pl.pallas_call(functools.partial(fused_kernel, sizes), out_shape=jax.Shap...  19.5 us
    unnamed x15, local copies, waits for them, and re-layouts  8.61 us

profile of v1, /device:TPU:0, one launch (start us, length us, event | category | flops | bytes accessed | tf_op | source)
XLA Modules:
  0.0 28.1 jit_solution(7096111579850845518)
XLA Ops:
  0.0 0.0 copy-start
  0.0 1.6 %copy-done = bf16[8,1024,128]{2,1,0:T(8,128)(2,1)S(1)} copy-done((bf16[8,1024,128]{2,1,0:T(8,128)(2,1)S(1)}, bf16[8,1024,128]{2,1,0:T(8,128)(2,1)}, u32[]{:S(2)}) %copy-start) | copy-done | bytes 2097176
  1.6 0.0 copy-start.1
  1.6 1.6 %copy-done.1 = f32[32,2,64,64]{3,2,1,0:T(8,128)S(1)} copy-done((f32[32,2,64,64]{3,2,1,0:T(8,128)S(1)}, f32[32,2,64,64]{3,2,1,0:T(8,128)}, u32[]{:S(2)}) %copy-start.1) | copy-done | bytes 1048600
  3.2 0.0 copy-start.2
  3.2 1.6 %copy-done.2 = bf16[2,512,1024]{2,1,0:T(8,128)(2,1)S(1)} copy-done((bf16[2,512,1024]{2,1,0:T(8,128)(2,1)S(1)}, bf16[2,512,1024]{2,1,0:T(8,128)(2,1)}, u32[]{:S(2)}) %copy-start.2) | copy-done | bytes 2097176
  4.8 0.0 copy-start.3
  4.8 1.2 %copy-done.3 = bf16[8,512,2,64]{1,3,2,0:T(8,128)(2,1)S(1)} copy-done((bf16[8,512,2,64]{1,3,2,0:T(8,128)(2,1)S(1)}, bf16[8,512,2,64]{1,3,2,0:T(8,128)(2,1)}, u32[]{:S(2)}) %copy-start.3) | copy-done | bytes 1048600
  6.0 0.0 copy-start.4
  6.0 0.7 %copy-done.4 = s32[3,8,2]{1,2,0:T(2,128)S(1)} copy-done((s32[3,8,2]{1,2,0:T(2,128)S(1)}, s32[3,8,2]{1,2,0:T(2,128)}, u32[]{:S(2)}) %copy-start.4) | copy-done | bytes 216
  6.7 0.0 copy-start.5
  6.7 0.7 %copy-done.5 = s32[128]{0:T(128)S(1)} copy-done((s32[128]{0:T(128)S(1)}, s32[128]{0:T(128)}, u32[]{:S(2)}) %copy-start.5) | copy-done | bytes 536
  7.3 0.0 copy-start.6
  7.3 0.7 %copy-done.6 = s32[128]{0:T(128)S(1)} copy-done((s32[128]{0:T(128)S(1)}, s32[128]{0:T(128)}, u32[]{:S(2)}) %copy-start.6) | copy-done | bytes 536
  8.0 19.5 %shard_map.73 = f32[1,2,32,128]{3,2,1,0:T(8,128)S(1)} custom-call(bf16[8,1024,128]{2,1,0:T(8,128)(2,1)S(1)} %copy-done, s32[1,128]{1,0:T(1,128)S(1)} %bitcast.8, s32[1,128]{1,0:T(1,128)S(1)} %bitcast.9, bf16[8,128,512]{2,1,0:T(8,128)(2,1)S(1)} %bitcast.6, bf16[2,512,1024]{2,1,0:T(8,128)(2,1)S(1)} %copy-done.2, f32[32,2,64,64]{3,2,1,0:T(8,128)S(1)} %copy-done.1, ...), custom_call_target="tpu_custom_call" | custom-call | tf_op jit(solution)/shard_map/pallas_call | solution.py:396
  27.5 0.6 %copy.9 = f32[1,2,32,128]{3,2,1,0:T(8,128)} copy(f32[1,2,32,128]{3,2,1,0:T(8,128)S(1)} %shard_map.73) | data formatting | bytes 65536
Async XLA Ops:
  0.0 1.6 %copy-start = (bf16[8,1024,128]{2,1,0:T(8,128)(2,1)S(1)}, bf16[8,1024,128]{2,1,0:T(8,128)(2,1)}, u32[]{:S(2)}) copy-start(bf16[8,1024,128]{2,1,0:T(8,128)(2,1)} %x_hbm.1) | copy-start | bytes 6291460
  1.6 1.6 %copy-start.1 = (f32[32,2,64,64]{3,2,1,0:T(8,128)S(1)}, f32[32,2,64,64]{3,2,1,0:T(8,128)}, u32[]{:S(2)}) copy-start(f32[32,2,64,64]{3,2,1,0:T(8,128)} %tr_hbm.1) | copy-start | bytes 3145732
  3.2 1.6 %copy-start.2 = (bf16[2,512,1024]{2,1,0:T(8,128)(2,1)S(1)}, bf16[2,512,1024]{2,1,0:T(8,128)(2,1)}, u32[]{:S(2)}) copy-start(bf16[2,512,1024]{2,1,0:T(8,128)(2,1)} %constant.2.clone.tab_hbm) | copy-start | bytes 6291460
  4.8 1.2 %copy-start.3 = (bf16[8,512,2,64]{1,3,2,0:T(8,128)(2,1)S(1)}, bf16[8,512,2,64]{1,3,2,0:T(8,128)(2,1)}, u32[]{:S(2)}) copy-start(bf16[8,512,2,64]{1,3,2,0:T(8,128)(2,1)} %param.10) | copy-start | bytes 3145732
  6.0 0.7 %copy-start.4 = (s32[3,8,2]{1,2,0:T(2,128)S(1)}, s32[3,8,2]{1,2,0:T(2,128)}, u32[]{:S(2)}) copy-start(s32[3,8,2]{1,2,0:T(2,128)} %param.12) | copy-start | bytes 580
  6.7 0.7 %copy-start.5 = (s32[128]{0:T(128)S(1)}, s32[128]{0:T(128)}, u32[]{:S(2)}) copy-start(s32[128]{0:T(128)} %param.8) | copy-start | bytes 1540
  7.3 0.7 %copy-start.6 = (s32[128]{0:T(128)S(1)}, s32[128]{0:T(128)}, u32[]{:S(2)}) copy-start(s32[128]{0:T(128)} %param.9) | copy-start | bytes 1540

commit v2 on v1

--- a/solution.py
+++ b/solution.py
@@ -152,13 +152,15 @@
 def fused_kernel(
     sizes,
     x_hbm,
-    low_ref,
-    high_ref,
+    low_hbm,
+    high_hbm,
     q_hbm,
     tab_hbm,
     tr_hbm,
+    level_hbm,
+    out_ref,
+    band_v,
     level_ref,
-    out_ref,
     x_v,
     q_v,
     tab_v,
@@ -171,6 +173,7 @@
     send2,
     recv2,
     load_sem,
+    small_sem,
     send_sem1,
     recv_sem1,
     send_sem2,
@@ -190,6 +193,11 @@
     half = rank // sub_count
     block = LANES // devices
 
+    band_loads = [
+        pltpu.make_async_copy(low_hbm, band_v.at[0], small_sem.at[0]),
+        pltpu.make_async_copy(high_hbm, band_v.at[1], small_sem.at[1]),
+    ]
+    level_load = pltpu.make_async_copy(level_hbm, level_ref, small_sem.at[2])
     loads = []
     for h in range(chunks):
         loads.append(pltpu.make_async_copy(tab_hbm.at[h], tab_v.at[h], load_sem.at[len(loads)]))
@@ -207,9 +215,12 @@
     loads[0].start()
     for load in x_loads:
         load.start()
+    for load in band_loads:
+        load.start()
     q_load.start()
     for load in loads[1:]:
         load.start()
+    level_load.start()
     tr_load.start()
 
     offsets = [
@@ -243,7 +254,10 @@
         loads[h].wait()
         width = bands * LANES
         freq = lax.broadcasted_iota(jnp.int32, (width, LANES), 0) + h * width
-        keep = (freq >= low_ref[...]) & (freq < high_ref[...])
+        if h == 0:
+            for load in band_loads:
+                load.wait()
+        keep = (freq >= band_v[0]) & (freq < band_v[1])
         for pair in range(pairs):
             if h == 0:
                 x_loads[2 * pair].wait()
@@ -288,6 +302,7 @@
             copy.start()
             copies1.append(copy)
 
+    level_load.wait()
     tr_load.wait()
     for level in range(levels):
         stride = 2**level
@@ -390,23 +405,17 @@
     weights = leaf_weights.transpose(0, 2, 3, 1).reshape(traces, 2 * rank, freq_total)
     block = shots // devices
     rows = sizes[0] // chunks * block
-    any_spec = pl.BlockSpec(memory_space=pl.ANY)
+    hbm_spec = pl.BlockSpec(memory_space=pltpu.HBM)
     vmem_spec = pl.BlockSpec(memory_space=pltpu.VMEM)
     dma = pltpu.SemaphoreType.DMA
     return pl.pallas_call(
         functools.partial(fused_kernel, sizes),
         out_shape=jax.ShapeDtypeStruct((1, 2, rank // sizes[2], shots), jnp.float32),
-        in_specs=[
-            any_spec,
-            vmem_spec,
-            vmem_spec,
-            any_spec,
-            any_spec,
-            any_spec,
-            pl.BlockSpec(memory_space=pltpu.SMEM),
-        ],
+        in_specs=[hbm_spec] * 7,
         out_specs=vmem_spec,
         scratch_shapes=[
+            pltpu.VMEM((2, 1, shots), jnp.int32),
+            pltpu.SMEM((levels, 2, boxes), jnp.int32),
             pltpu.VMEM((traces // 2, samples, 2 * shots), jnp.bfloat16),
             pltpu.VMEM(weights.shape, jnp.bfloat16),
             pltpu.VMEM(table.shape, jnp.bfloat16),
@@ -419,13 +428,14 @@
             pltpu.VMEM((boxes // 2 * sizes[2], block, LANES), jnp.float32),
             pltpu.VMEM((devices, block, LANES), jnp.float32),
             dma((chunks + traces + 2,)),
+            dma((3,)),
             dma((chunks, devices - 1)),
             dma((chunks, devices - 1)),
             dma((devices - 1,)),
             dma((devices - 1,)),
         ],
         compiler_params=pltpu.CompilerParams(
-            collective_id=0, has_side_effects=True, vmem_limit_bytes=40 * 2**20
+            collective_id=0, has_side_effects=True, vmem_limit_bytes=56 * 2**20
         ),
     )(
         seismic,

time: 28.4 us -> 21.4 us (0.75)
  local copies, waits for them, and re-layouts: 8.61 us -> 1.38 us
  Pallas kernels: 19.5 us -> 19.9 us
    unnamed x15 -> x1, local copies, waits for them, and re-layouts: 8.61 us -> 1.38 us
    pallas_call x1, Pallas kernels: 19.5 us -> 19.9 us  [fused_device(): pl.pallas_call(functools.partial(fused_kernel, sizes), out_shape=jax.Shap...]
where the time goes in v2:
time: 21.4 us; the launch traced here: 21.3 us
  Pallas kernels  19.9 us (93%)
  local copies, waits for them, and re-layouts  1.38 us (6%)
    pallas_call x1, Pallas kernels, fused_device(): pl.pallas_call(functools.partial(fused_kernel, sizes), out_shape=jax.Shap...  19.9 us
    unnamed x1, local copies, waits for them, and re-layouts  1.38 us

profile of v2, /device:TPU:0, one launch (start us, length us, event | category | flops | bytes accessed | tf_op | source)
XLA Modules:
  0.0 21.3 jit_solution(8949286698789537460)
XLA Ops:
  0.0 19.9 %shard_map.73 = f32[1,2,32,128]{3,2,1,0:T(8,128)} custom-call(bf16[8,1024,128]{2,1,0:T(8,128)(2,1)} %x_hbm.1, s32[1,128]{1,0:T(1,128)} %bitcast.8, s32[1,128]{1,0:T(1,128)} %bitcast.9, bf16[8,128,512]{2,1,0:T(8,128)(2,1)} %bitcast.6, bf16[2,512,1024]{2,1,0:T(8,128)(2,1)} %constant.2.clone.tab_hbm, f32[32,2,64,64]{3,2,1,0:T(8,128)} %tr_hbm.1, s32[3,2,8]{2,1,0:T(2,128)} %bitcast.7), custom_call_target="tpu_custom_call" | custom-call | tf_op jit(solution)/shard_map/pallas_call | solution.py:411
  19.9 1.4 %copy.9 = f32[1,2,32,128]{3,2,1,0:T(8,128)} copy(f32[1,2,32,128]{3,2,1,0:T(8,128)} %shard_map.73) | data formatting | bytes 65536

commit v3 on v2

--- a/solution.py
+++ b/solution.py
@@ -249,9 +249,39 @@
             device_id_type=pl.DeviceIdType.MESH,
         )
 
+    def place_matrices(level, q):
+        stride = 2**level
+        lower = [b for b in range(boxes) if b // stride % 2 == 0][q]
+        for side in range(2):
+            for child in range(2):
+                entry = level_ref[level, child, lower + side * stride]
+                real, imag = tr_v[entry, 0], tr_v[entry, 1]
+                top = jnp.concatenate([real, -imag], axis=1)
+                bottom = jnp.concatenate([imag, real], axis=1)
+                columns = slice(child * LANES, (child + 1) * LANES)
+                for part, rows in enumerate((top, bottom)):
+                    high, rest = split_two(rows)
+                    high, rest = high.astype(jnp.bfloat16), rest.astype(jnp.bfloat16)
+                    if level < levels - 1:
+                        at = side * 2 * rank + part * rank
+                        mat_hi[level, q, at : at + rank, columns] = high
+                        mat_lo[level, q, at : at + rank, columns] = rest
+                    else:
+                        for s in range(sub_count):
+                            at = s * 4 * half + side * 2 * half + part * half
+                            mine = slice(s * half, (s + 1) * half)
+                            mat_hi[level, q, at : at + half, columns] = high[mine]
+                            mat_lo[level, q, at : at + half, columns] = rest[mine]
+
+    to_place = [(level, q) for level in range(levels) for q in range(boxes // 2)]
+    per_pair = -(-len(to_place) // pairs)
+
     copies1 = []
     for h in range(chunks):
         loads[h].wait()
+        if h == chunks - 1:
+            level_load.wait()
+            tr_load.wait()
         width = bands * LANES
         freq = lax.broadcasted_iota(jnp.int32, (width, LANES), 0) + h * width
         if h == 0:
@@ -262,6 +292,9 @@
             if h == 0:
                 x_loads[2 * pair].wait()
                 x_loads[2 * pair + 1].wait()
+            if h == chunks - 1:
+                for level, q in to_place[pair * per_pair : (pair + 1) * per_pair]:
+                    place_matrices(level, q)
             rows = jnp.dot(tab_v[h], x_v[pair], preferred_element_type=jnp.float32)
             for part in range(2):
                 for k in range(2):
@@ -302,33 +335,6 @@
             copy.start()
             copies1.append(copy)
 
-    level_load.wait()
-    tr_load.wait()
-    for level in range(levels):
-        stride = 2**level
-        lowers = [b for b in range(boxes) if b // stride % 2 == 0]
-        for q, lower in enumerate(lowers):
-            for side in range(2):
-                for child in range(2):
-                    entry = level_ref[level, child, lower + side * stride]
-                    real, imag = tr_v[entry, 0], tr_v[entry, 1]
-                    top = jnp.concatenate([real, -imag], axis=1)
-                    bottom = jnp.concatenate([imag, real], axis=1)
-                    for part, rows in enumerate((top, bottom)):
-                        high, rest = split_two(rows)
-                        high, rest = high.astype(jnp.bfloat16), rest.astype(jnp.bfloat16)
-                        columns = slice(child * LANES, (child + 1) * LANES)
-                        if level < levels - 1:
-                            at = side * 2 * rank + part * rank
-                            mat_hi[level, q, at : at + rank, columns] = high
-                            mat_lo[level, q, at : at + rank, columns] = rest
-                        else:
-                            for s in range(sub_count):
-                                at = s * 4 * half + side * 2 * half + part * half
-                                mine = slice(s * half, (s + 1) * half)
-                                mat_hi[level, q, at : at + half, columns] = high[mine]
-                                mat_lo[level, q, at : at + half, columns] = rest[mine]
-
     same = [send1[h, me].astype(jnp.float32) for h in range(chunks)]
     other = [None] * chunks
     for h in range(chunks):
@@ -366,13 +372,18 @@
                 now[lower], now[lower + stride] = joined[:, :LANES], joined[:, LANES:]
             else:
                 for s in range(sub_count):
-                    send2[q * sub_count + s] = joined[:, s * LANES : (s + 1) * LANES]
+                    for side in range(2):
+                        at = s * LANES + side * 2 * half
+                        mine = joined[:, at : at + 2 * half]
+                        send2[(q + side * len(lowers)) * sub_count + s] = jnp.concatenate(
+                            [mine[: block // 2], mine[block // 2 :]], axis=1
+                        )
 
     copies2 = []
     for i, offset in enumerate(offsets):
         tt, pp, uu = place(offset)
         copy = pltpu.make_async_remote_copy(
-            src_ref=send2.at[lax.rem(tt * space_count + pp, boxes // 2) * sub_count + uu],
+            src_ref=send2.at[(tt * space_count + pp) * sub_count + uu],
             dst_ref=recv2.at[me],
             send_sem=send_sem2.at[i],
             recv_sem=recv_sem2.at[i],
@@ -381,14 +392,14 @@
         )
         copy.start()
         copies2.append(copy)
-    mine = t * space_count + p
-    recv2[me] = send2[lax.rem(mine, boxes // 2) * sub_count + u]
+    recv2[me] = send2[me]
     for copy in copies2:
         copy.wait_recv()
-    turned = recv2[...].reshape(LANES, LANES).T
-    upper = mine >= boxes // 2
-    chosen = jnp.where(upper, turned[2 * half :], turned[: 2 * half])
-    out_ref[...] = chosen.reshape(1, 2, half, LANES)
+    pieces = []
+    for d in range(devices):
+        got = recv2[d]
+        pieces += [got[:, : 2 * half], got[:, 2 * half :]]
+    out_ref[...] = jnp.concatenate(pieces, axis=0).T.reshape(1, 2, half, LANES)
     for copy in copies1 + copies2:
         copy.wait_send()
 
@@ -425,8 +436,8 @@
             pltpu.VMEM((levels, boxes // 2, 4 * rank, 4 * rank), jnp.bfloat16),
             pltpu.VMEM((chunks, devices, rows, LANES), jnp.bfloat16),
             pltpu.VMEM((chunks, devices - 1, rows, LANES), jnp.bfloat16),
-            pltpu.VMEM((boxes // 2 * sizes[2], block, LANES), jnp.float32),
-            pltpu.VMEM((devices, block, LANES), jnp.float32),
+            pltpu.VMEM((devices, block // 2, LANES), jnp.float32),
+            pltpu.VMEM((devices, block // 2, LANES), jnp.float32),
             dma((chunks + traces + 2,)),
             dma((3,)),
             dma((chunks, devices - 1)),

time: 21.4 us -> 21.5 us (level)
  no operation moved by 1% of the time
where the time goes in v3:
time: 21.5 us; the launch traced here: 21.3 us
  Pallas kernels  19.9 us (93%)
  local copies, waits for them, and re-layouts  1.38 us (6%)
    pallas_call x1, Pallas kernels, fused_device(): pl.pallas_call(functools.partial(fused_kernel, sizes), out_shape=jax.Shap...  19.9 us
    unnamed x1, local copies, waits for them, and re-layouts  1.38 us

profile of v3, /device:TPU:0, one launch (start us, length us, event | category | flops | bytes accessed | tf_op | source)
XLA Modules:
  0.0 21.3 jit_solution(16324469370238435653)
XLA Ops:
  0.0 19.9 %shard_map.73 = f32[1,2,32,128]{3,2,1,0:T(8,128)} custom-call(bf16[8,1024,128]{2,1,0:T(8,128)(2,1)} %x_hbm.1, s32[1,128]{1,0:T(1,128)} %bitcast.8, s32[1,128]{1,0:T(1,128)} %bitcast.9, bf16[8,128,512]{2,1,0:T(8,128)(2,1)} %bitcast.6, bf16[2,512,1024]{2,1,0:T(8,128)(2,1)} %constant.2.clone.tab_hbm, f32[32,2,64,64]{3,2,1,0:T(8,128)} %tr_hbm.1, s32[3,2,8]{2,1,0:T(2,128)} %bitcast.7), custom_call_target="tpu_custom_call" | custom-call | tf_op jit(solution)/shard_map/pallas_call | solution.py:422
  19.9 1.4 %copy.9 = f32[1,2,32,128]{3,2,1,0:T(8,128)} copy(f32[1,2,32,128]{3,2,1,0:T(8,128)} %shard_map.73) | data formatting | bytes 65536

commit v4 on v3

--- a/solution.py
+++ b/solution.py
@@ -168,6 +168,7 @@
     spec_v,
     mat_hi,
     mat_lo,
+    stage,
     send1,
     recv1,
     send2,
@@ -201,20 +202,19 @@
     loads = []
     for h in range(chunks):
         loads.append(pltpu.make_async_copy(tab_hbm.at[h], tab_v.at[h], load_sem.at[len(loads)]))
-    x_loads = []
-    for j in range(traces):
-        x_loads.append(
-            pltpu.make_async_copy(
-                x_hbm.at[j],
-                x_v.at[j // 2, :, pl.ds(j % 2 * LANES, LANES)],
-                load_sem.at[chunks + j],
-            )
+
+    def x_load(pair, k):
+        return pltpu.make_async_copy(
+            x_hbm.at[2 * pair + k],
+            x_v.at[pair, :, pl.ds(k * LANES, LANES)],
+            load_sem.at[chunks + 2 * pair + k],
         )
+
     q_load = pltpu.make_async_copy(q_hbm, q_v, load_sem.at[chunks + traces])
     tr_load = pltpu.make_async_copy(tr_hbm, tr_v, load_sem.at[chunks + traces + 1])
     loads[0].start()
-    for load in x_loads:
-        load.start()
+    for j in range(traces):
+        x_load(j // 2, j % 2).start()
     for load in band_loads:
         load.start()
     q_load.start()
@@ -223,35 +223,24 @@
     level_load.start()
     tr_load.start()
 
-    offsets = [
-        (dt, dp, du)
-        for dt in range(trace_count)
-        for dp in range(space_count)
-        for du in range(sub_count)
-        if dt or dp or du
-    ]
-    offsets.sort(key=lambda o: -min(o[0], trace_count - o[0]) * 4 - o[1] * 2 - o[2])
-
-    def place(offset):
-        dt, dp, du = offset
-        tt = lax.rem(t + dt, trace_count)
-        pp = lax.rem(p + dp, space_count)
-        uu = lax.rem(u + du, sub_count)
-        return tt, pp, uu
+    def place(i):
+        tt = lax.rem(t + i // (space_count * sub_count), trace_count)
+        pp = lax.rem(p + i // sub_count % space_count, space_count)
+        uu = lax.rem(u + i % sub_count, sub_count)
+        return (tt * space_count + pp) * sub_count + uu, {"trace": tt, "space": pp, "sub": uu}
 
     barrier = pltpu.get_barrier_semaphore()
-    for offset in offsets:
-        tt, pp, uu = place(offset)
+
+    @pl.loop(1, devices)
+    def _(i):
+        _, target = place(i)
         pl.semaphore_signal(
-            barrier,
-            inc=1,
-            device_id={"trace": tt, "space": pp, "sub": uu},
-            device_id_type=pl.DeviceIdType.MESH,
+            barrier, inc=1, device_id=target, device_id_type=pl.DeviceIdType.MESH
         )
 
     def place_matrices(level, q):
         stride = 2**level
-        lower = [b for b in range(boxes) if b // stride % 2 == 0][q]
+        lower = q // stride * (2 * stride) + q % stride
         for side in range(2):
             for child in range(2):
                 entry = level_ref[level, child, lower + side * stride]
@@ -273,78 +262,94 @@
                             mat_hi[level, q, at : at + half, columns] = high[mine]
                             mat_lo[level, q, at : at + half, columns] = rest[mine]
 
-    to_place = [(level, q) for level in range(levels) for q in range(boxes // 2)]
-    per_pair = -(-len(to_place) // pairs)
-
-    copies1 = []
+    def copy1(h, i):
+        d, target = place(i)
+        return pltpu.make_async_remote_copy(
+            src_ref=send1.at[h, d],
+            dst_ref=recv1.at[h, i],
+            send_sem=send_sem1.at[h, i],
+            recv_sem=recv_sem1.at[h, i],
+            device_id=target,
+            device_id_type=pl.DeviceIdType.MESH,
+        )
+
+    def copy2(i):
+        d, target = place(i)
+        return pltpu.make_async_remote_copy(
+            src_ref=send2.at[d],
+            dst_ref=recv2.at[me],
+            send_sem=send_sem2.at[i],
+            recv_sem=recv_sem2.at[i],
+            device_id=target,
+            device_id_type=pl.DeviceIdType.MESH,
+        )
+
+    width = bands * LANES
     for h in range(chunks):
         loads[h].wait()
+        if h == 0:
+            for load in band_loads:
+                load.wait()
         if h == chunks - 1:
             level_load.wait()
             tr_load.wait()
-        width = bands * LANES
-        freq = lax.broadcasted_iota(jnp.int32, (width, LANES), 0) + h * width
-        if h == 0:
-            for load in band_loads:
-                load.wait()
-        keep = (freq >= band_v[0]) & (freq < band_v[1])
-        for pair in range(pairs):
+
+        @pl.loop(0, pairs)
+        def _(pair, h=h):
             if h == 0:
-                x_loads[2 * pair].wait()
-                x_loads[2 * pair + 1].wait()
+                for k in range(2):
+                    x_load(pair, k).wait()
             if h == chunks - 1:
-                for level, q in to_place[pair * per_pair : (pair + 1) * per_pair]:
-                    place_matrices(level, q)
+                for level in range(levels):
+                    place_matrices(level, pair)
             rows = jnp.dot(tab_v[h], x_v[pair], preferred_element_type=jnp.float32)
+            freq = lax.broadcasted_iota(jnp.int32, (width, LANES), 0) + h * width
+            keep = (freq >= band_v[0]) & (freq < band_v[1])
             for part in range(2):
                 for k in range(2):
                     piece = rows[part * width : (part + 1) * width, k * LANES : (k + 1) * LANES]
                     piece = jnp.where(keep, piece, 0.0).astype(jnp.bfloat16)
-                    j = 2 * pair + k
                     for g in range(bands):
-                        spec_v[
-                            h * bands + g,
-                            j * LANES : (j + 1) * LANES,
-                            part * LANES : (part + 1) * LANES,
-                        ] = piece[g * LANES : (g + 1) * LANES]
+                        columns = slice(part * LANES, (part + 1) * LANES)
+                        spec_v[h * bands + g, 2 * pair + k, :, columns] = piece[
+                            g * LANES : (g + 1) * LANES
+                        ]
+
         if h == 0:
             q_load.wait()
-        leaves = []
-        for g in range(h * bands, (h + 1) * bands):
-            left = jnp.concatenate(
-                [q_v[j, :, g * LANES : (g + 1) * LANES] for j in range(traces)], axis=1
-            )
-            both = jnp.dot(left, spec_v[g], preferred_element_type=jnp.float32)
+
+        @pl.loop(0, bands)
+        def _(g, h=h):
+            band = h * bands + g
+            at = pl.ds(pl.multiple_of(band * LANES, LANES), LANES)
+            left = jnp.concatenate([q_v[j, :, at] for j in range(traces)], axis=1)
+            right = spec_v[band].reshape(traces * LANES, 2 * LANES)
+            both = jnp.dot(left, right, preferred_element_type=jnp.float32)
             real = both[:rank, :LANES] - both[rank:, LANES:]
             imag = both[rank:, :LANES] + both[:rank, LANES:]
             turned = jnp.concatenate([real, imag], axis=0).T
-            leaves.append(turned.reshape(devices, block, LANES))
-        send1[h] = jnp.concatenate(leaves, axis=1).astype(jnp.bfloat16)
+            stage[:, pl.ds(pl.multiple_of(g * block, block), block), :] = turned.reshape(
+                devices, block, LANES
+            )
+
+        send1[h] = stage[...].astype(jnp.bfloat16)
         if h == 0:
             pl.semaphore_wait(barrier, devices - 1)
-        for i, offset in enumerate(offsets):
-            tt, pp, uu = place(offset)
-            copy = pltpu.make_async_remote_copy(
-                src_ref=send1.at[h, (tt * space_count + pp) * sub_count + uu],
-                dst_ref=recv1.at[h, i],
-                send_sem=send_sem1.at[h, i],
-                recv_sem=recv_sem1.at[h, i],
-                device_id={"trace": tt, "space": pp, "sub": uu},
-                device_id_type=pl.DeviceIdType.MESH,
-            )
-            copy.start()
-            copies1.append(copy)
-
-    same = [send1[h, me].astype(jnp.float32) for h in range(chunks)]
-    other = [None] * chunks
-    for h in range(chunks):
-        for i, offset in enumerate(offsets):
-            copies1[h * len(offsets) + i].wait_recv()
-            got = recv1[h, i].astype(jnp.float32)
-            if offset[1] == 0:
-                same[h] = same[h] + got
-            else:
-                other[h] = got if other[h] is None else other[h] + got
+
+        @pl.loop(1, devices)
+        def _(i, h=h):
+            copy1(h, i).start()
+
+    def arrived(n, totals, dp):
+        i = n // sub_count * (space_count * sub_count) + dp * sub_count + n % sub_count
+        for h in range(chunks):
+            copy1(h, i).wait_recv()
+        return tuple(totals[h] + recv1[h, i].astype(jnp.float32) for h in range(chunks))
+
+    same = tuple(send1[h, me].astype(jnp.float32) for h in range(chunks))
+    same = lax.fori_loop(1, trace_count * sub_count, functools.partial(arrived, dp=0), same)
+    other = tuple(jnp.zeros_like(part) for part in same)
+    other = lax.fori_loop(0, trace_count * sub_count, functools.partial(arrived, dp=1), other)
     first = p == 0
     now = [None] * boxes
     for h in range(chunks):
@@ -379,29 +384,27 @@
                             [mine[: block // 2], mine[block // 2 :]], axis=1
                         )
 
-    copies2 = []
-    for i, offset in enumerate(offsets):
-        tt, pp, uu = place(offset)
-        copy = pltpu.make_async_remote_copy(
-            src_ref=send2.at[(tt * space_count + pp) * sub_count + uu],
-            dst_ref=recv2.at[me],
-            send_sem=send_sem2.at[i],
-            recv_sem=recv_sem2.at[i],
-            device_id={"trace": tt, "space": pp, "sub": uu},
-            device_id_type=pl.DeviceIdType.MESH,
-        )
-        copy.start()
-        copies2.append(copy)
+    @pl.loop(1, devices)
+    def _(i):
+        copy2(i).start()
+
     recv2[me] = send2[me]
-    for copy in copies2:
-        copy.wait_recv()
+
+    @pl.loop(1, devices)
+    def _(i):
+        copy2(i).wait_recv()
+
     pieces = []
     for d in range(devices):
         got = recv2[d]
         pieces += [got[:, : 2 * half], got[:, 2 * half :]]
     out_ref[...] = jnp.concatenate(pieces, axis=0).T.reshape(1, 2, half, LANES)
-    for copy in copies1 + copies2:
-        copy.wait_send()
+
+    @pl.loop(1, devices)
+    def _(i):
+        for h in range(chunks):
+            copy1(h, i).wait_send()
+        copy2(i).wait_send()
 
 
 def fused_device(seismic, band_low, band_high, leaf_weights, translations, level_table):
@@ -431,19 +434,20 @@
             pltpu.VMEM(weights.shape, jnp.bfloat16),
             pltpu.VMEM(table.shape, jnp.bfloat16),
             pltpu.VMEM(translations.shape, jnp.float32),
-            pltpu.VMEM((sizes[0], traces * LANES, 2 * LANES), jnp.bfloat16),
+            pltpu.VMEM((sizes[0], traces, LANES, 2 * LANES), jnp.bfloat16),
             pltpu.VMEM((levels, boxes // 2, 4 * rank, 4 * rank), jnp.bfloat16),
             pltpu.VMEM((levels, boxes // 2, 4 * rank, 4 * rank), jnp.bfloat16),
+            pltpu.VMEM((devices, rows, LANES), jnp.float32),
             pltpu.VMEM((chunks, devices, rows, LANES), jnp.bfloat16),
-            pltpu.VMEM((chunks, devices - 1, rows, LANES), jnp.bfloat16),
+            pltpu.VMEM((chunks, devices, rows, LANES), jnp.bfloat16),
             pltpu.VMEM((devices, block // 2, LANES), jnp.float32),
             pltpu.VMEM((devices, block // 2, LANES), jnp.float32),
             dma((chunks + traces + 2,)),
             dma((3,)),
-            dma((chunks, devices - 1)),
-            dma((chunks, devices - 1)),
-            dma((devices - 1,)),
-            dma((devices - 1,)),
+            dma((chunks, devices)),
+            dma((chunks, devices)),
+            dma((devices,)),
+            dma((devices,)),
         ],
         compiler_params=pltpu.CompilerParams(
             collective_id=0, has_side_effects=True, vmem_limit_bytes=56 * 2**20
@@ -473,6 +477,7 @@
         and 2 * rank == LANES
         and 4 * rank == LANES * sub_count
         and traces % 2 == 0
+        and space_count == 2
         and trace_count % 2 == 0
     )
     chosen = fused_device if fits else general_device

time: 21.5 us -> 22.2 us (1.033)
  Pallas kernels: 19.9 us -> 20.6 us
    pallas_call x1, Pallas kernels: 19.9 us -> 20.6 us  [fused_device(): pl.pallas_call(functools.partial(fused_kernel, sizes), out_shape=jax.Shap...]
where the time goes in v4:
time: 22.2 us; the launch traced here: 22 us
  Pallas kernels  20.6 us (93%)
  local copies, waits for them, and re-layouts  1.38 us (6%)
    pallas_call x1, Pallas kernels, fused_device(): pl.pallas_call(functools.partial(fused_kernel, sizes), out_shape=jax.Shap...  20.6 us
    unnamed x1, local copies, waits for them, and re-layouts  1.38 us

profile of v4, /device:TPU:0, one launch (start us, length us, event | category | flops | bytes accessed | tf_op | source)
XLA Modules:
  0.0 22.0 jit_solution(12177278721302644485)
XLA Ops:
  0.0 20.6 %shard_map.73 = f32[1,2,32,128]{3,2,1,0:T(8,128)} custom-call(bf16[8,1024,128]{2,1,0:T(8,128)(2,1)} %x_hbm.1, s32[1,128]{1,0:T(1,128)} %bitcast.8, s32[1,128]{1,0:T(1,128)} %bitcast.9, bf16[8,128,512]{2,1,0:T(8,128)(2,1)} %bitcast.6, bf16[2,512,1024]{2,1,0:T(8,128)(2,1)} %constant.2.clone.tab_hbm, f32[32,2,64,64]{3,2,1,0:T(8,128)} %tr_hbm.1, s32[3,2,8]{2,1,0:T(2,128)} %bitcast.7), custom_call_target="tpu_custom_call" | custom-call | tf_op jit(solution)/shard_map/pallas_call | solution.py:425
  20.7 1.4 %copy.9 = f32[1,2,32,128]{3,2,1,0:T(8,128)} copy(f32[1,2,32,128]{3,2,1,0:T(8,128)} %shard_map.73) | data formatting | bytes 65536

commit v5 on v3

--- a/solution.py
+++ b/solution.py
@@ -168,16 +168,12 @@
     spec_v,
     mat_hi,
     mat_lo,
-    send1,
-    recv1,
-    send2,
-    recv2,
+    send,
+    recv,
     load_sem,
     small_sem,
-    send_sem1,
-    recv_sem1,
-    send_sem2,
-    recv_sem2,
+    send_sem,
+    recv_sem,
 ):
     trace_count, space_count, sub_count = sizes
     devices = trace_count * space_count * sub_count
@@ -191,7 +187,6 @@
     levels = mat_hi.shape[0]
     rank = tr_v.shape[2]
     half = rank // sub_count
-    block = LANES // devices
 
     band_loads = [
         pltpu.make_async_copy(low_hbm, band_v.at[0], small_sem.at[0]),
@@ -253,30 +248,22 @@
         stride = 2**level
         lower = [b for b in range(boxes) if b // stride % 2 == 0][q]
         for side in range(2):
-            for child in range(2):
-                entry = level_ref[level, child, lower + side * stride]
+            for child in range(2 if level else 1):
+                entry = level_ref[level, child if level else p, lower + side * stride]
                 real, imag = tr_v[entry, 0], tr_v[entry, 1]
+                columns = slice(child * LANES, (child + 1) * LANES)
                 top = jnp.concatenate([real, -imag], axis=1)
                 bottom = jnp.concatenate([imag, real], axis=1)
-                columns = slice(child * LANES, (child + 1) * LANES)
                 for part, rows in enumerate((top, bottom)):
                     high, rest = split_two(rows)
-                    high, rest = high.astype(jnp.bfloat16), rest.astype(jnp.bfloat16)
-                    if level < levels - 1:
-                        at = side * 2 * rank + part * rank
-                        mat_hi[level, q, at : at + rank, columns] = high
-                        mat_lo[level, q, at : at + rank, columns] = rest
-                    else:
-                        for s in range(sub_count):
-                            at = s * 4 * half + side * 2 * half + part * half
-                            mine = slice(s * half, (s + 1) * half)
-                            mat_hi[level, q, at : at + half, columns] = high[mine]
-                            mat_lo[level, q, at : at + half, columns] = rest[mine]
+                    at = (side * 2 + part) * rank
+                    mat_hi[level, q, at : at + rank, columns] = high.astype(jnp.bfloat16)
+                    mat_lo[level, q, at : at + rank, columns] = rest.astype(jnp.bfloat16)
 
     to_place = [(level, q) for level in range(levels) for q in range(boxes // 2)]
     per_pair = -(-len(to_place) // pairs)
 
-    copies1 = []
+    leaves = []
     for h in range(chunks):
         loads[h].wait()
         if h == chunks - 1:
@@ -309,7 +296,6 @@
                         ] = piece[g * LANES : (g + 1) * LANES]
         if h == 0:
             q_load.wait()
-        leaves = []
         for g in range(h * bands, (h + 1) * bands):
             left = jnp.concatenate(
                 [q_v[j, :, g * LANES : (g + 1) * LANES] for j in range(traces)], axis=1
@@ -317,90 +303,63 @@
             both = jnp.dot(left, spec_v[g], preferred_element_type=jnp.float32)
             real = both[:rank, :LANES] - both[rank:, LANES:]
             imag = both[rank:, :LANES] + both[:rank, LANES:]
-            turned = jnp.concatenate([real, imag], axis=0).T
-            leaves.append(turned.reshape(devices, block, LANES))
-        send1[h] = jnp.concatenate(leaves, axis=1).astype(jnp.bfloat16)
-        if h == 0:
-            pl.semaphore_wait(barrier, devices - 1)
-        for i, offset in enumerate(offsets):
-            tt, pp, uu = place(offset)
-            copy = pltpu.make_async_remote_copy(
-                src_ref=send1.at[h, (tt * space_count + pp) * sub_count + uu],
-                dst_ref=recv1.at[h, i],
-                send_sem=send_sem1.at[h, i],
-                recv_sem=recv_sem1.at[h, i],
-                device_id={"trace": tt, "space": pp, "sub": uu},
-                device_id_type=pl.DeviceIdType.MESH,
-            )
-            copy.start()
-            copies1.append(copy)
-
-    same = [send1[h, me].astype(jnp.float32) for h in range(chunks)]
-    other = [None] * chunks
-    for h in range(chunks):
-        for i, offset in enumerate(offsets):
-            copies1[h * len(offsets) + i].wait_recv()
-            got = recv1[h, i].astype(jnp.float32)
-            if offset[1] == 0:
-                same[h] = same[h] + got
-            else:
-                other[h] = got if other[h] is None else other[h] + got
-    first = p == 0
+            leaves.append(jnp.concatenate([real, imag], axis=0))
+
+    def apply(level, q, packed):
+        depth = packed.shape[0]
+        main = jnp.dot(mat_hi[level, q, :, :depth], packed, preferred_element_type=jnp.float32)
+        rest = jnp.dot(
+            mat_lo[level, q, :, :depth], packed[:, :LANES], preferred_element_type=jnp.float32
+        )
+        return main[:, :LANES] + (main[:, LANES:] + rest)
+
+    def packed_two(value):
+        return jnp.concatenate(split_two(value), axis=1).astype(jnp.bfloat16)
+
     now = [None] * boxes
-    for h in range(chunks):
-        for place_no in range(space_count):
-            total = jnp.where(first == (place_no == 0), same[h], other[h])
-            for g in range(bands):
-                box = (h * bands + g) * space_count + place_no
-                now[box] = total[g * block : (g + 1) * block]
-
     for level in range(levels):
         stride = 2**level
         lowers = [b for b in range(boxes) if b // stride % 2 == 0]
+        before = now[:]
         for q, lower in enumerate(lowers):
-            both = jnp.concatenate([now[lower], now[lower + stride]], axis=1)
-            left = jnp.concatenate(split_two(both), axis=0).astype(jnp.bfloat16)
-            dims = (((1,), (1,)), ((), ()))
-            main = lax.dot_general(
-                left, mat_hi[level, q], dims, preferred_element_type=jnp.float32
-            )
-            rest = lax.dot_general(
-                left, mat_lo[level, q], dims, preferred_element_type=jnp.float32
-            )
-            joined = main[:block] + (main[block:] + rest[:block])
-            if level < levels - 1:
-                now[lower], now[lower + stride] = joined[:, :LANES], joined[:, LANES:]
+            if level == 0:
+                packed = packed_two(leaves[q])
             else:
-                for s in range(sub_count):
-                    for side in range(2):
-                        at = s * LANES + side * 2 * half
-                        mine = joined[:, at : at + 2 * half]
-                        send2[(q + side * len(lowers)) * sub_count + s] = jnp.concatenate(
-                            [mine[: block // 2], mine[block // 2 :]], axis=1
-                        )
-
-    copies2 = []
+                packed = jnp.concatenate([before[lower], before[lower + stride]], axis=0)
+            both = apply(level, q, packed)
+            for side in range(2):
+                mine = both[side * LANES : (side + 1) * LANES]
+                box = lower + side * stride
+                if level < levels - 1:
+                    now[box] = packed_two(mine)
+                else:
+                    for s in range(sub_count):
+                        for part in range(2):
+                            at = part * rank + s * half
+                            send[box * sub_count + s, part * half : (part + 1) * half] = mine[
+                                at : at + half
+                            ].astype(jnp.bfloat16)
+
+    pl.semaphore_wait(barrier, devices - 1)
+    copies = []
     for i, offset in enumerate(offsets):
         tt, pp, uu = place(offset)
         copy = pltpu.make_async_remote_copy(
-            src_ref=send2.at[(tt * space_count + pp) * sub_count + uu],
-            dst_ref=recv2.at[me],
-            send_sem=send_sem2.at[i],
-            recv_sem=recv_sem2.at[i],
+            src_ref=send.at[(tt * space_count + pp) * sub_count + uu],
+            dst_ref=recv.at[i],
+            send_sem=send_sem.at[i],
+            recv_sem=recv_sem.at[i],
             device_id={"trace": tt, "space": pp, "sub": uu},
             device_id_type=pl.DeviceIdType.MESH,
         )
         copy.start()
-        copies2.append(copy)
-    recv2[me] = send2[me]
-    for copy in copies2:
-        copy.wait_recv()
-    pieces = []
-    for d in range(devices):
-        got = recv2[d]
-        pieces += [got[:, : 2 * half], got[:, 2 * half :]]
-    out_ref[...] = jnp.concatenate(pieces, axis=0).T.reshape(1, 2, half, LANES)
-    for copy in copies1 + copies2:
+        copies.append(copy)
+    total = send[me].astype(jnp.float32)
+    for i in reversed(range(len(offsets))):
+        copies[i].wait_recv()
+        total = total + recv[i].astype(jnp.float32)
+    out_ref[...] = total.reshape(1, 2, half, LANES)
+    for copy in copies:
         copy.wait_send()
 
 
@@ -414,8 +373,7 @@
     levels = level_table.shape[0]
     table = jnp.asarray(table_rows(freq_total, samples, chunks))
     weights = leaf_weights.transpose(0, 2, 3, 1).reshape(traces, 2 * rank, freq_total)
-    block = shots // devices
-    rows = sizes[0] // chunks * block
+    half = rank // sizes[2]
     hbm_spec = pl.BlockSpec(memory_space=pltpu.HBM)
     vmem_spec = pl.BlockSpec(memory_space=pltpu.VMEM)
     dma = pltpu.SemaphoreType.DMA
@@ -434,14 +392,10 @@
             pltpu.VMEM((sizes[0], traces * LANES, 2 * LANES), jnp.bfloat16),
             pltpu.VMEM((levels, boxes // 2, 4 * rank, 4 * rank), jnp.bfloat16),
             pltpu.VMEM((levels, boxes // 2, 4 * rank, 4 * rank), jnp.bfloat16),
-            pltpu.VMEM((chunks, devices, rows, LANES), jnp.bfloat16),
-            pltpu.VMEM((chunks, devices - 1, rows, LANES), jnp.bfloat16),
-            pltpu.VMEM((devices, block // 2, LANES), jnp.float32),
-            pltpu.VMEM((devices, block // 2, LANES), jnp.float32),
+            pltpu.VMEM((devices, 2 * half, shots), jnp.bfloat16),
+            pltpu.VMEM((devices - 1, 2 * half, shots), jnp.bfloat16),
             dma((chunks + traces + 2,)),
             dma((3,)),
-            dma((chunks, devices - 1)),
-            dma((chunks, devices - 1)),
             dma((devices - 1,)),
             dma((devices - 1,)),
         ],
@@ -468,10 +422,9 @@
     freq_total, rank = leaf_weights.shape[1], leaf_weights.shape[3]
     fits = (
         shots == LANES
-        and shots == 8 * devices
         and freq_total == trace_count * LANES
         and 2 * rank == LANES
-        and 4 * rank == LANES * sub_count
+        and space_count == 2
         and traces % 2 == 0
         and trace_count % 2 == 0
     )

time: 21.5 us -> 20 us (0.930)
  Pallas kernels: 19.9 us -> 18.5 us
    pallas_call x1, Pallas kernels: 19.9 us -> 18.5 us  [fused_device(): pl.pallas_call(functools.partial(fused_kernel, sizes), out_shape=jax.Shap...]
where the time goes in v5:
time: 20 us; the launch traced here: 19.8 us
  Pallas kernels  18.5 us (92%)
  local copies, waits for them, and re-layouts  1.38 us (7%)
    pallas_call x1, Pallas kernels, fused_device(): pl.pallas_call(functools.partial(fused_kernel, sizes), out_shape=jax.Shap...  18.5 us
    unnamed x1, local copies, waits for them, and re-layouts  1.38 us

profile of v5, /device:TPU:0, one launch (start us, length us, event | category | flops | bytes accessed | tf_op | source)
XLA Modules:
  0.0 19.8 jit_solution(7077620113175590423)
XLA Ops:
  0.0 18.5 %shard_map.73 = f32[1,2,32,128]{3,2,1,0:T(8,128)} custom-call(bf16[8,1024,128]{2,1,0:T(8,128)(2,1)} %x_hbm.1, s32[1,128]{1,0:T(1,128)} %bitcast.8, s32[1,128]{1,0:T(1,128)} %bitcast.9, bf16[8,128,512]{2,1,0:T(8,128)(2,1)} %bitcast.6, bf16[2,512,1024]{2,1,0:T(8,128)(2,1)} %constant.2.clone.tab_hbm, f32[32,2,64,64]{3,2,1,0:T(8,128)} %tr_hbm.1, s32[3,2,8]{2,1,0:T(2,128)} %bitcast.7), custom_call_target="tpu_custom_call" | custom-call | tf_op jit(solution)/shard_map/pallas_call | solution.py:380
  18.5 1.4 %copy.9 = f32[1,2,32,128]{3,2,1,0:T(8,128)} copy(f32[1,2,32,128]{3,2,1,0:T(8,128)} %shard_map.73) | data formatting | bytes 65536

commit v6 on v5

--- a/solution.py
+++ b/solution.py
@@ -168,17 +168,20 @@
     spec_v,
     mat_hi,
     mat_lo,
+    own,
+    give,
+    near,
     send,
     recv,
     load_sem,
     small_sem,
+    near_send_sem,
+    near_recv_sem,
     send_sem,
     recv_sem,
 ):
     trace_count, space_count, sub_count = sizes
-    devices = trace_count * space_count * sub_count
     t, p, u = lax.axis_index("trace"), lax.axis_index("space"), lax.axis_index("sub")
-    me = (t * space_count + p) * sub_count + u
     chunks = tab_v.shape[0]
     traces = q_v.shape[0]
     pairs = traces // 2
@@ -219,28 +222,24 @@
     tr_load.start()
 
     offsets = [
-        (dt, dp, du)
-        for dt in range(trace_count)
-        for dp in range(space_count)
-        for du in range(sub_count)
-        if dt or dp or du
+        (dt, dp) for dt in range(trace_count) for dp in range(space_count) if dt or dp
     ]
-    offsets.sort(key=lambda o: -min(o[0], trace_count - o[0]) * 4 - o[1] * 2 - o[2])
+    offsets.sort(key=lambda o: -min(o[0], trace_count - o[0]) * 2 - o[1])
 
     def place(offset):
-        dt, dp, du = offset
-        tt = lax.rem(t + dt, trace_count)
-        pp = lax.rem(p + dp, space_count)
-        uu = lax.rem(u + du, sub_count)
-        return tt, pp, uu
-
+        return lax.rem(t + offset[0], trace_count), lax.rem(p + offset[1], space_count)
+
+    sibling = {"sub": 1 - u}
     barrier = pltpu.get_barrier_semaphore()
+    pl.semaphore_signal(
+        barrier, inc=1, device_id=sibling, device_id_type=pl.DeviceIdType.MESH
+    )
     for offset in offsets:
-        tt, pp, uu = place(offset)
+        tt, pp = place(offset)
         pl.semaphore_signal(
             barrier,
             inc=1,
-            device_id={"trace": tt, "space": pp, "sub": uu},
+            device_id={"trace": tt, "space": pp},
             device_id_type=pl.DeviceIdType.MESH,
         )
 
@@ -316,8 +315,20 @@
     def packed_two(value):
         return jnp.concatenate(split_two(value), axis=1).astype(jnp.bfloat16)
 
+    def near_copy(box):
+        return pltpu.make_async_remote_copy(
+            src_ref=give.at[box],
+            dst_ref=near.at[box],
+            send_sem=near_send_sem.at[box],
+            recv_sem=near_recv_sem.at[box],
+            device_id=sibling,
+            device_id_type=pl.DeviceIdType.MESH,
+        )
+
     now = [None] * boxes
     for level in range(levels):
+        if level == levels - 1:
+            pl.semaphore_wait(barrier, len(offsets) + 1)
         stride = 2**level
         lowers = [b for b in range(boxes) if b // stride % 2 == 0]
         before = now[:]
@@ -333,39 +344,47 @@
                 if level < levels - 1:
                     now[box] = packed_two(mine)
                 else:
-                    for s in range(sub_count):
-                        for part in range(2):
-                            at = part * rank + s * half
-                            send[box * sub_count + s, part * half : (part + 1) * half] = mine[
-                                at : at + half
-                            ].astype(jnp.bfloat16)
-
-    pl.semaphore_wait(barrier, devices - 1)
+                    for part in range(2):
+                        first, second = (
+                            mine[part * rank + s * half : part * rank + (s + 1) * half]
+                            for s in range(2)
+                        )
+                        rows = slice(part * half, (part + 1) * half)
+                        own[box, rows] = jnp.where(u == 0, first, second)
+                        give[box, rows] = jnp.where(u == 0, second, first).astype(jnp.bfloat16)
+                    near_copy(box).start()
+
+    def summed(box):
+        near_copy(box).wait_recv()
+        return own[box] + near[box].astype(jnp.float32)
+
     copies = []
     for i, offset in enumerate(offsets):
-        tt, pp, uu = place(offset)
+        tt, pp = place(offset)
+        send[i] = summed(tt * space_count + pp).astype(jnp.bfloat16)
         copy = pltpu.make_async_remote_copy(
-            src_ref=send.at[(tt * space_count + pp) * sub_count + uu],
+            src_ref=send.at[i],
             dst_ref=recv.at[i],
             send_sem=send_sem.at[i],
             recv_sem=recv_sem.at[i],
-            device_id={"trace": tt, "space": pp, "sub": uu},
+            device_id={"trace": tt, "space": pp},
             device_id_type=pl.DeviceIdType.MESH,
         )
         copy.start()
         copies.append(copy)
-    total = send[me].astype(jnp.float32)
+    total = summed(t * space_count + p)
     for i in reversed(range(len(offsets))):
         copies[i].wait_recv()
         total = total + recv[i].astype(jnp.float32)
     out_ref[...] = total.reshape(1, 2, half, LANES)
+    for box in range(boxes):
+        near_copy(box).wait_send()
     for copy in copies:
         copy.wait_send()
 
 
 def fused_device(seismic, band_low, band_high, leaf_weights, translations, level_table):
     sizes = tuple(lax.axis_size(name) for name in ("trace", "space", "sub"))
-    devices = math.prod(sizes)
     boxes = sizes[0] * sizes[1]
     traces, samples, shots = seismic.shape
     freq_total, rank = leaf_weights.shape[1], leaf_weights.shape[3]
@@ -392,12 +411,17 @@
             pltpu.VMEM((sizes[0], traces * LANES, 2 * LANES), jnp.bfloat16),
             pltpu.VMEM((levels, boxes // 2, 4 * rank, 4 * rank), jnp.bfloat16),
             pltpu.VMEM((levels, boxes // 2, 4 * rank, 4 * rank), jnp.bfloat16),
-            pltpu.VMEM((devices, 2 * half, shots), jnp.bfloat16),
-            pltpu.VMEM((devices - 1, 2 * half, shots), jnp.bfloat16),
+            pltpu.VMEM((boxes, 2 * half, shots), jnp.float32),
+            pltpu.VMEM((boxes, 2 * half, shots), jnp.bfloat16),
+            pltpu.VMEM((boxes, 2 * half, shots), jnp.bfloat16),
+            pltpu.VMEM((boxes - 1, 2 * half, shots), jnp.bfloat16),
+            pltpu.VMEM((boxes - 1, 2 * half, shots), jnp.bfloat16),
             dma((chunks + traces + 2,)),
             dma((3,)),
-            dma((devices - 1,)),
-            dma((devices - 1,)),
+            dma((boxes,)),
+            dma((boxes,)),
+            dma((boxes - 1,)),
+            dma((boxes - 1,)),
         ],
         compiler_params=pltpu.CompilerParams(
             collective_id=0, has_side_effects=True, vmem_limit_bytes=56 * 2**20
@@ -417,7 +441,6 @@
     trace_count, space_count, sub_count = (
         lax.axis_size(name) for name in ("trace", "space", "sub")
     )
-    devices = trace_count * space_count * sub_count
     traces, _, shots = seismic.shape
     freq_total, rank = leaf_weights.shape[1], leaf_weights.shape[3]
     fits = (
@@ -425,6 +448,7 @@
         and freq_total == trace_count * LANES
         and 2 * rank == LANES
         and space_count == 2
+        and sub_count == 2
         and traces % 2 == 0
         and trace_count % 2 == 0
     )

time: 20 us -> 19.4 us (0.970)
  Pallas kernels: 18.5 us -> 17.8 us
    pallas_call x1, Pallas kernels: 18.5 us -> 17.8 us  [fused_device(): pl.pallas_call(functools.partial(fused_kernel, sizes), out_shape=jax.Shap...]
where the time goes in v6:
time: 19.4 us; the launch traced here: 19.2 us
  Pallas kernels  17.8 us (92%)
  local copies, waits for them, and re-layouts  1.38 us (7%)
    pallas_call x1, Pallas kernels, fused_device(): pl.pallas_call(functools.partial(fused_kernel, sizes), out_shape=jax.Shap...  17.8 us
    unnamed x1, local copies, waits for them, and re-layouts  1.38 us

profile of v6, /device:TPU:0, one launch (start us, length us, event | category | flops | bytes accessed | tf_op | source)
XLA Modules:
  0.0 19.2 jit_solution(12358478890198777445)
XLA Ops:
  0.0 17.8 %shard_map.73 = f32[1,2,32,128]{3,2,1,0:T(8,128)} custom-call(bf16[8,1024,128]{2,1,0:T(8,128)(2,1)} %x_hbm.1, s32[1,128]{1,0:T(1,128)} %bitcast.8, s32[1,128]{1,0:T(1,128)} %bitcast.9, bf16[8,128,512]{2,1,0:T(8,128)(2,1)} %bitcast.6, bf16[2,512,1024]{2,1,0:T(8,128)(2,1)} %constant.2.clone.tab_hbm, f32[32,2,64,64]{3,2,1,0:T(8,128)} %tr_hbm.1, s32[3,2,8]{2,1,0:T(2,128)} %bitcast.7), custom_call_target="tpu_custom_call" | custom-call | tf_op jit(solution)/shard_map/pallas_call | solution.py:399
  17.8 1.4 %copy.9 = f32[1,2,32,128]{3,2,1,0:T(8,128)} copy(f32[1,2,32,128]{3,2,1,0:T(8,128)} %shard_map.73) | data formatting | bytes 65536

commit v7 on v6

--- a/solution.py
+++ b/solution.py
@@ -196,30 +196,27 @@
         pltpu.make_async_copy(high_hbm, band_v.at[1], small_sem.at[1]),
     ]
     level_load = pltpu.make_async_copy(level_hbm, level_ref, small_sem.at[2])
-    loads = []
-    for h in range(chunks):
-        loads.append(pltpu.make_async_copy(tab_hbm.at[h], tab_v.at[h], load_sem.at[len(loads)]))
+    slabs = 4
+    slab = tab_v.shape[1] // slabs
+    tab_loads = [
+        pltpu.make_async_copy(
+            tab_hbm.at[0, pl.ds(n * slab, slab)], tab_v.at[0, pl.ds(n * slab, slab)], load_sem.at[n]
+        )
+        for n in range(slabs)
+    ]
     x_loads = []
     for j in range(traces):
         x_loads.append(
             pltpu.make_async_copy(
                 x_hbm.at[j],
                 x_v.at[j // 2, :, pl.ds(j % 2 * LANES, LANES)],
-                load_sem.at[chunks + j],
+                load_sem.at[slabs + j],
             )
         )
-    q_load = pltpu.make_async_copy(q_hbm, q_v, load_sem.at[chunks + traces])
-    tr_load = pltpu.make_async_copy(tr_hbm, tr_v, load_sem.at[chunks + traces + 1])
-    loads[0].start()
-    for load in x_loads:
+    q_load = pltpu.make_async_copy(q_hbm, q_v, load_sem.at[slabs + traces])
+    tr_load = pltpu.make_async_copy(tr_hbm, tr_v, load_sem.at[slabs + traces + 1])
+    for load in band_loads + x_loads[:2] + tab_loads + x_loads[2:] + [level_load]:
         load.start()
-    for load in band_loads:
-        load.start()
-    q_load.start()
-    for load in loads[1:]:
-        load.start()
-    level_load.start()
-    tr_load.start()
 
     offsets = [
         (dt, dp) for dt in range(trace_count) for dp in range(space_count) if dt or dp
@@ -260,14 +257,12 @@
                     mat_lo[level, q, at : at + rank, columns] = rest.astype(jnp.bfloat16)
 
     to_place = [(level, q) for level in range(levels) for q in range(boxes // 2)]
-    per_pair = -(-len(to_place) // pairs)
+    per_pair = -(-len(to_place) // (pairs - 1))
 
     leaves = []
     for h in range(chunks):
-        loads[h].wait()
-        if h == chunks - 1:
-            level_load.wait()
-            tr_load.wait()
+        for load in tab_loads:
+            load.wait()
         width = bands * LANES
         freq = lax.broadcasted_iota(jnp.int32, (width, LANES), 0) + h * width
         if h == 0:
@@ -275,11 +270,16 @@
                 load.wait()
         keep = (freq >= band_v[0]) & (freq < band_v[1])
         for pair in range(pairs):
-            if h == 0:
-                x_loads[2 * pair].wait()
-                x_loads[2 * pair + 1].wait()
-            if h == chunks - 1:
-                for level, q in to_place[pair * per_pair : (pair + 1) * per_pair]:
+            x_loads[2 * pair].wait()
+            x_loads[2 * pair + 1].wait()
+            if pair == 0:
+                tr_load.start()
+                q_load.start()
+            if pair == 1:
+                level_load.wait()
+                tr_load.wait()
+            if pair >= 1:
+                for level, q in to_place[(pair - 1) * per_pair : pair * per_pair]:
                     place_matrices(level, q)
             rows = jnp.dot(tab_v[h], x_v[pair], preferred_element_type=jnp.float32)
             for part in range(2):
@@ -293,8 +293,7 @@
                             j * LANES : (j + 1) * LANES,
                             part * LANES : (part + 1) * LANES,
                         ] = piece[g * LANES : (g + 1) * LANES]
-        if h == 0:
-            q_load.wait()
+        q_load.wait()
         for g in range(h * bands, (h + 1) * bands):
             left = jnp.concatenate(
                 [q_v[j, :, g * LANES : (g + 1) * LANES] for j in range(traces)], axis=1
@@ -388,7 +387,7 @@
     boxes = sizes[0] * sizes[1]
     traces, samples, shots = seismic.shape
     freq_total, rank = leaf_weights.shape[1], leaf_weights.shape[3]
-    chunks = 2
+    chunks = 1
     levels = level_table.shape[0]
     table = jnp.asarray(table_rows(freq_total, samples, chunks))
     weights = leaf_weights.transpose(0, 2, 3, 1).reshape(traces, 2 * rank, freq_total)
@@ -416,7 +415,7 @@
             pltpu.VMEM((boxes, 2 * half, shots), jnp.bfloat16),
             pltpu.VMEM((boxes - 1, 2 * half, shots), jnp.bfloat16),
             pltpu.VMEM((boxes - 1, 2 * half, shots), jnp.bfloat16),
-            dma((chunks + traces + 2,)),
+            dma((traces + 6,)),
             dma((3,)),
             dma((boxes,)),
             dma((boxes,)),
@@ -450,6 +449,7 @@
         and space_count == 2
         and sub_count == 2
         and traces % 2 == 0
+        and traces > 2
         and trace_count % 2 == 0
     )
     chosen = fused_device if fits else general_device

time: 19.4 us -> 20.5 us (1.057)
  Pallas kernels: 17.8 us -> 19 us
    pallas_call x1, Pallas kernels: 17.8 us -> 19 us  [fused_device(): pl.pallas_call(functools.partial(fused_kernel, sizes), out_shape=jax.Shap...]
where the time goes in v7:
time: 20.5 us; the launch traced here: 20.3 us
  Pallas kernels  19 us (93%)
  local copies, waits for them, and re-layouts  1.38 us (7%)
    pallas_call x1, Pallas kernels, fused_device(): pl.pallas_call(functools.partial(fused_kernel, sizes), out_shape=jax.Shap...  19 us
    unnamed x1, local copies, waits for them, and re-layouts  1.38 us

profile of v7, /device:TPU:0, one launch (start us, length us, event | category | flops | bytes accessed | tf_op | source)
XLA Modules:
  0.0 20.3 jit_solution(5309025163925244220)
XLA Ops:
  0.0 19.0 %shard_map.73 = f32[1,2,32,128]{3,2,1,0:T(8,128)} custom-call(bf16[8,1024,128]{2,1,0:T(8,128)(2,1)} %x_hbm.1, s32[1,128]{1,0:T(1,128)} %bitcast.8, s32[1,128]{1,0:T(1,128)} %bitcast.9, bf16[8,128,512]{2,1,0:T(8,128)(2,1)} %bitcast.6, bf16[1,1024,1024]{2,1,0:T(8,128)(2,1)} %constant.2.clone.tab_hbm, f32[32,2,64,64]{3,2,1,0:T(8,128)} %tr_hbm.1, s32[3,2,8]{2,1,0:T(2,128)} %bitcast.7), custom_call_target="tpu_custom_call" | custom-call | tf_op jit(solution)/shard_map/pallas_call | solution.py:398
  19.0 1.4 %copy.9 = f32[1,2,32,128]{3,2,1,0:T(8,128)} copy(f32[1,2,32,128]{3,2,1,0:T(8,128)} %shard_map.73) | data formatting | bytes 65536

commit v8 on v6

--- a/solution.py
+++ b/solution.py
@@ -196,30 +196,33 @@
         pltpu.make_async_copy(high_hbm, band_v.at[1], small_sem.at[1]),
     ]
     level_load = pltpu.make_async_copy(level_hbm, level_ref, small_sem.at[2])
-    loads = []
+    slabs = 4
+    slab = tab_v.shape[1] // slabs
+    tab_loads = []
     for h in range(chunks):
-        loads.append(pltpu.make_async_copy(tab_hbm.at[h], tab_v.at[h], load_sem.at[len(loads)]))
+        for n in range(slabs):
+            rows = pl.ds(n * slab, slab)
+            tab_loads.append(
+                pltpu.make_async_copy(
+                    tab_hbm.at[h, rows], tab_v.at[h, rows], load_sem.at[len(tab_loads)]
+                )
+            )
     x_loads = []
     for j in range(traces):
         x_loads.append(
             pltpu.make_async_copy(
                 x_hbm.at[j],
                 x_v.at[j // 2, :, pl.ds(j % 2 * LANES, LANES)],
-                load_sem.at[chunks + j],
+                load_sem.at[chunks * slabs + j],
             )
         )
-    q_load = pltpu.make_async_copy(q_hbm, q_v, load_sem.at[chunks + traces])
-    tr_load = pltpu.make_async_copy(tr_hbm, tr_v, load_sem.at[chunks + traces + 1])
-    loads[0].start()
-    for load in x_loads:
+    q_load = pltpu.make_async_copy(q_hbm, q_v, load_sem.at[chunks * slabs + traces])
+    tr_load = pltpu.make_async_copy(tr_hbm, tr_v, load_sem.at[chunks * slabs + traces + 1])
+    for load in band_loads + x_loads[:2] + tab_loads[:slabs] + x_loads[2:] + tab_loads[slabs:]:
         load.start()
-    for load in band_loads:
-        load.start()
+    tr_load.start()
+    level_load.start()
     q_load.start()
-    for load in loads[1:]:
-        load.start()
-    level_load.start()
-    tr_load.start()
 
     offsets = [
         (dt, dp) for dt in range(trace_count) for dp in range(space_count) if dt or dp
@@ -260,14 +263,13 @@
                     mat_lo[level, q, at : at + rank, columns] = rest.astype(jnp.bfloat16)
 
     to_place = [(level, q) for level in range(levels) for q in range(boxes // 2)]
-    per_pair = -(-len(to_place) // pairs)
+    late = pairs // 2
+    per_pair = -(-len(to_place) // late)
 
     leaves = []
     for h in range(chunks):
-        loads[h].wait()
-        if h == chunks - 1:
-            level_load.wait()
-            tr_load.wait()
+        for load in tab_loads[h * slabs : (h + 1) * slabs]:
+            load.wait()
         width = bands * LANES
         freq = lax.broadcasted_iota(jnp.int32, (width, LANES), 0) + h * width
         if h == 0:
@@ -278,8 +280,12 @@
             if h == 0:
                 x_loads[2 * pair].wait()
                 x_loads[2 * pair + 1].wait()
-            if h == chunks - 1:
-                for level, q in to_place[pair * per_pair : (pair + 1) * per_pair]:
+            if h == chunks - 1 and pair >= pairs - late:
+                if pair == pairs - late:
+                    level_load.wait()
+                    tr_load.wait()
+                done = (pair - pairs + late) * per_pair
+                for level, q in to_place[done : done + per_pair]:
                     place_matrices(level, q)
             rows = jnp.dot(tab_v[h], x_v[pair], preferred_element_type=jnp.float32)
             for part in range(2):
@@ -293,16 +299,15 @@
                             j * LANES : (j + 1) * LANES,
                             part * LANES : (part + 1) * LANES,
                         ] = piece[g * LANES : (g + 1) * LANES]
-        if h == 0:
-            q_load.wait()
-        for g in range(h * bands, (h + 1) * bands):
-            left = jnp.concatenate(
-                [q_v[j, :, g * LANES : (g + 1) * LANES] for j in range(traces)], axis=1
-            )
-            both = jnp.dot(left, spec_v[g], preferred_element_type=jnp.float32)
-            real = both[:rank, :LANES] - both[rank:, LANES:]
-            imag = both[rank:, :LANES] + both[:rank, LANES:]
-            leaves.append(jnp.concatenate([real, imag], axis=0))
+    q_load.wait()
+    for g in range(trace_count):
+        left = jnp.concatenate(
+            [q_v[j, :, g * LANES : (g + 1) * LANES] for j in range(traces)], axis=1
+        )
+        both = jnp.dot(left, spec_v[g], preferred_element_type=jnp.float32)
+        real = both[:rank, :LANES] - both[rank:, LANES:]
+        imag = both[rank:, :LANES] + both[:rank, LANES:]
+        leaves.append(jnp.concatenate([real, imag], axis=0))
 
     def apply(level, q, packed):
         depth = packed.shape[0]
@@ -416,7 +421,7 @@
             pltpu.VMEM((boxes, 2 * half, shots), jnp.bfloat16),
             pltpu.VMEM((boxes - 1, 2 * half, shots), jnp.bfloat16),
             pltpu.VMEM((boxes - 1, 2 * half, shots), jnp.bfloat16),
-            dma((chunks + traces + 2,)),
+            dma((4 * chunks + traces + 2,)),
             dma((3,)),
             dma((boxes,)),
             dma((boxes,)),

time: 19.4 us -> 19.6 us (1.010)
  Pallas kernels: 17.8 us -> 18.1 us
    pallas_call x1, Pallas kernels: 17.8 us -> 18.1 us  [fused_device(): pl.pallas_call(functools.partial(fused_kernel, sizes), out_shape=jax.Shap...]
where the time goes in v8:
time: 19.6 us; the launch traced here: 19.4 us
  Pallas kernels  18.1 us (92%)
  local copies, waits for them, and re-layouts  1.38 us (7%)
    pallas_call x1, Pallas kernels, fused_device(): pl.pallas_call(functools.partial(fused_kernel, sizes), out_shape=jax.Shap...  18.1 us
    unnamed x1, local copies, waits for them, and re-layouts  1.38 us

profile of v8, /device:TPU:0, one launch (start us, length us, event | category | flops | bytes accessed | tf_op | source)
XLA Modules:
  0.0 19.4 jit_solution(1854912217605960213)
XLA Ops:
  0.0 18.1 %shard_map.73 = f32[1,2,32,128]{3,2,1,0:T(8,128)} custom-call(bf16[8,1024,128]{2,1,0:T(8,128)(2,1)} %x_hbm.1, s32[1,128]{1,0:T(1,128)} %bitcast.8, s32[1,128]{1,0:T(1,128)} %bitcast.9, bf16[8,128,512]{2,1,0:T(8,128)(2,1)} %bitcast.6, bf16[2,512,1024]{2,1,0:T(8,128)(2,1)} %constant.2.clone.tab_hbm, f32[32,2,64,64]{3,2,1,0:T(8,128)} %tr_hbm.1, s32[3,2,8]{2,1,0:T(2,128)} %bitcast.7), custom_call_target="tpu_custom_call" | custom-call | tf_op jit(solution)/shard_map/pallas_call | solution.py:404
  18.1 1.4 %copy.9 = f32[1,2,32,128]{3,2,1,0:T(8,128)} copy(f32[1,2,32,128]{3,2,1,0:T(8,128)} %shard_map.73) | data formatting | bytes 65536

commit v9 on v8

--- a/solution.py
+++ b/solution.py
@@ -287,10 +287,14 @@
                 done = (pair - pairs + late) * per_pair
                 for level, q in to_place[done : done + per_pair]:
                     place_matrices(level, q)
-            rows = jnp.dot(tab_v[h], x_v[pair], preferred_element_type=jnp.float32)
             for part in range(2):
+                rows = jnp.dot(
+                    tab_v[h, part * width : (part + 1) * width],
+                    x_v[pair],
+                    preferred_element_type=jnp.float32,
+                )
                 for k in range(2):
-                    piece = rows[part * width : (part + 1) * width, k * LANES : (k + 1) * LANES]
+                    piece = rows[:, k * LANES : (k + 1) * LANES]
                     piece = jnp.where(keep, piece, 0.0).astype(jnp.bfloat16)
                     j = 2 * pair + k
                     for g in range(bands):

time: 19.6 us -> 18.6 us (0.949)
  Pallas kernels: 18.1 us -> 17.1 us
    pallas_call x1, Pallas kernels: 18.1 us -> 17.1 us  [fused_device(): pl.pallas_call(functools.partial(fused_kernel, sizes), out_shape=jax.Shap...]
where the time goes in v9:
time: 18.6 us; the launch traced here: 18.5 us
  Pallas kernels  17.1 us (92%)
  local copies, waits for them, and re-layouts  1.38 us (7%)
    pallas_call x1, Pallas kernels, fused_device(): pl.pallas_call(functools.partial(fused_kernel, sizes), out_shape=jax.Shap...  17.1 us
    unnamed x1, local copies, waits for them, and re-layouts  1.38 us

profile of v9, /device:TPU:0, one launch (start us, length us, event | category | flops | bytes accessed | tf_op | source)
XLA Modules:
  0.0 18.5 jit_solution(11388786786874530905)
XLA Ops:
  0.0 17.1 %shard_map.73 = f32[1,2,32,128]{3,2,1,0:T(8,128)} custom-call(bf16[8,1024,128]{2,1,0:T(8,128)(2,1)} %x_hbm.1, s32[1,128]{1,0:T(1,128)} %bitcast.8, s32[1,128]{1,0:T(1,128)} %bitcast.9, bf16[8,128,512]{2,1,0:T(8,128)(2,1)} %bitcast.6, bf16[2,512,1024]{2,1,0:T(8,128)(2,1)} %constant.2.clone.tab_hbm, f32[32,2,64,64]{3,2,1,0:T(8,128)} %tr_hbm.1, s32[3,2,8]{2,1,0:T(2,128)} %bitcast.7), custom_call_target="tpu_custom_call" | custom-call | tf_op jit(solution)/shard_map/pallas_call | solution.py:408
  17.1 1.4 %copy.9 = f32[1,2,32,128]{3,2,1,0:T(8,128)} copy(f32[1,2,32,128]{3,2,1,0:T(8,128)} %shard_map.73) | data formatting | bytes 65536
